TPU v7x, 256 devices: a whole 4x4x8 slice. The times are simulated.
256 devices in a mesh: row: 32 (over z_hi, y, core), col: 8 (over z_lo, x).
Axes of the slice: x: 4, y: 4, z: 8 (z_hi: 4, z_lo: 2; z = z_hi * 2 + z_lo), core: 2. Of those that a mesh axis runs over, the one named last changes fastest.
Arguments:
- holograms: float32 [4, 4096, 4096], P(None, 'row', 'col'), may hold values from -6 to 6
- fresnel: float32 [4], replicated, may hold values from 0.01 to 0.05
- ctf_terms: float32 [2], replicated, may hold values from 0.1 to 0.6
Outputs:
- phase: float32 [4096, 4096], P('row', 'col')
All inputs are finite; a program needn't handle non-finite values.
Results may differ from a plain program's by a relative error of at most 0.0003.
Values sent between devices are 32-bit elements; how exact they have to be, the bound alone decides.
No kernel may reach another device: no remote copies, remote signals or barrier semaphores. Data moves between devices by JAX's collectives and lax.ppermute only.
A program may use at most 128 MiB of HBM per device.

v0:
```python
import math

import jax
import jax.numpy as jnp
import ml_dtypes
import numpy as np
from jax import lax
from jax.experimental import pallas as pl
from jax.experimental.pallas import tpu as pltpu
from jax.sharding import PartitionSpec as P

N = 4096
POS, NEG, ZERO, HALF = range(4)
F32 = jnp.float32
BF16 = jnp.bfloat16


def residues(quad):
    low, high = 2 * quad, 2 * quad + 1
    if quad == 0:
        return [0, 1, 16, 31]
    return [low, high, 32 - low, 32 - high]


def member(kind, group, slot):
    if kind == POS:
        return 4 * group + slot
    if kind == NEG:
        return 127 - 4 * group - slot
    if kind == ZERO:
        return [2 * group, 2 * group + 1, 128 - 2 * group if group else 64, 127 - 2 * group][slot]
    return [2 * group, 2 * group + 1, 127 - 2 * group, 126 - 2 * group][slot]


def halves(matrix):
    high = matrix.astype(ml_dtypes.bfloat16)
    low = (matrix - high.astype(np.float64)).astype(ml_dtypes.bfloat16)
    return np.stack([high, low])


def turn(product, length):
    angle = 2.0 * np.pi * (np.asarray(product, np.int64) % length) / length
    return np.cos(angle), np.sin(angle)


def row_constants():
    mats = []
    for kind in range(4):
        k2 = np.array([[member(kind, g, s) for s in range(4)] for g in range(32)])
        cosine, sine = turn(k2[:, :, None] * np.arange(128), 128)
        real = np.concatenate([cosine, sine], -1)
        imag = np.concatenate([-sine, cosine], -1)
        both = np.stack([real.reshape(32, 2, 2, 256), imag.reshape(32, 2, 2, 256)], 2)
        mats.append(halves(both.reshape(256, 256)))
    twist = np.stack(turn(np.arange(32)[:, None] * np.arange(128), N)).astype(np.float32)
    return np.stack(mats), twist


def column_constants():
    cosine, sine = turn(np.arange(16)[:, None] * np.arange(16), 16)
    eye8 = np.eye(8)
    forward = np.block(
        [
            [np.kron(eye8, cosine), np.kron(eye8, -sine)],
            [np.kron(eye8, sine), np.kron(eye8, cosine)],
        ]
    )
    pick = np.kron(np.eye(4), np.ones((2, 1)))
    twice = np.ones((1, 2))

    def spread(block):
        return np.kron(twice, np.kron(pick, block))

    inverse = np.block([[spread(cosine), spread(sine)], [spread(-sine), spread(cosine)]])
    lane = np.arange(128)
    within = lane % 16
    top = lane // 64
    step = np.arange(128)[None, :, None] + 128 * np.arange(2)[:, None, None]
    ahead = np.stack(turn(step * within, N)).astype(np.float32)
    step = np.arange(64)[None, :, None] + 128 * np.arange(2)[:, None, None] + 64 * top
    behind = np.stack(turn(step * within, N)).astype(np.float32)
    step = np.arange(2)[:, None, None] + 2 * top
    spin = np.stack(turn(step * np.arange(64)[None, :, None], 256)).astype(np.float32)
    return halves(forward), halves(inverse), ahead, np.stack([behind, spin])


def image_constants():
    mats = []
    for kind in range(4):
        k2 = np.array([[member(kind, g, s) for g in range(32)] for s in range(4)])
        k2 = k2.reshape(2, 2, 32).transpose(0, 2, 1).reshape(2, 64)
        cosine, sine = turn(np.arange(128)[:, None, None] * k2, 128)
        real = np.stack([cosine, -sine], 2).reshape(128, 256)
        imag = np.stack([sine, cosine], 2).reshape(128, 256)
        mats.append(halves(np.concatenate([real, imag])))
    lane = np.arange(256)
    quad = 4 * (lane // 128) + 2 * (lane // 64 % 2) + lane // 8 % 2
    k1 = np.array([residues(q)[s] for q, s in zip(quad, lane // 16 % 4)])
    twist = np.stack(turn(np.arange(128)[:, None] * k1, N)).astype(np.float32)
    cosine, sine = turn(np.arange(32)[:, None] * k1, 32)
    same = (np.arange(8)[:, None] == lane % 8).astype(np.float64)
    real = np.concatenate([cosine[:, None] * same, -sine[:, None] * same], -1)
    imag = np.concatenate([sine[:, None] * same, cosine[:, None] * same], -1)
    last = np.concatenate([real, imag], 1).reshape(512, 512) * (0.5 / (N * N))
    return np.stack(mats), twist, halves(last)


def turned(value, angle_index, length, sign):
    angle_index %= length
    real, imag = value
    if angle_index == 0:
        return value
    if 4 * angle_index == length:
        return (-imag, real) if sign > 0 else (imag, -real)
    if 2 * angle_index == length:
        return (-real, -imag)
    if 4 * angle_index == 3 * length:
        return (imag, -real) if sign > 0 else (-imag, real)
    angle = sign * 2.0 * math.pi * angle_index / length
    cosine, sine = math.cos(angle), math.sin(angle)
    if (8 * angle_index) % length == 0:
        scale = abs(cosine)
        plus, minus = (real + imag) * scale, (real - imag) * scale
        if cosine > 0:
            return (minus, plus) if sine > 0 else (plus, -minus)
        return (-plus, minus) if sine > 0 else (-minus, -plus)
    return (real * cosine - imag * sine, imag * cosine + real * sine)


def plus(a, b):
    return (a[0] + b[0], a[1] + b[1])


def minus(a, b):
    return (a[0] - b[0], a[1] - b[1])


def transform(values, sign):
    length = len(values)
    if length == 1:
        return values
    if length == 2:
        return [plus(values[0], values[1]), minus(values[0], values[1])]
    quarter = length // 4
    columns = []
    for b in range(quarter):
        z0, z1, z2, z3 = (values[a * quarter + b] for a in range(4))
        even, odd = plus(z0, z2), plus(z1, z3)
        even_gap, odd_gap = minus(z0, z2), turned(minus(z1, z3), 1, 4, sign)
        outs = [plus(even, odd), plus(even_gap, odd_gap), minus(even, odd), minus(even_gap, odd_gap)]
        columns.append([turned(z, b * k, length, sign) for k, z in enumerate(outs)])
    result = [None] * length
    for k in range(4):
        for m, z in enumerate(transform([columns[b][k] for b in range(quarter)], sign)):
            result[k + 4 * m] = z
    return result


def times(value, cosine, sine):
    real, imag = value
    return (real * cosine - imag * sine, imag * cosine + real * sine)


def split(value):
    high = value.astype(BF16)
    return high, (value - high.astype(F32)).astype(BF16)


def product(left, right, dims):
    def one(a, b):
        return lax.dot_general(a, b, (dims, ((), ())), preferred_element_type=F32)

    return one(left[0], right[0]) + (one(left[0], right[1]) + one(left[1], right[0]))


def rows_kernel(field_ref, mats_ref, twist_ref, out_ref, high_ref, low_ref):
    for j in range(2):
        lines = []
        for n1 in range(32):
            at = pl.ds(128 * (n1 % 4), 128)
            lines.append(
                (field_ref[n1 // 4, 2 * j, :, at], field_ref[n1 // 4, 2 * j + 1, :, at])
            )
        lines = transform(lines, -1)
        for quad in range(8):
            for slot, k1 in enumerate(residues(quad)):
                line = lines[k1]
                if k1:
                    line = times(line, twist_ref[0, pl.ds(k1, 1), :], -twist_ref[1, pl.ds(k1, 1), :])
                rows = pl.ds(128 * quad + 32 * slot + 16 * j, 16)
                for part in range(2):
                    high, low = split(line[part])
                    high_ref[rows, pl.ds(128 * part, 128)] = high
                    low_ref[rows, pl.ds(128 * part, 128)] = low
    lane = lax.broadcasted_iota(jnp.int32, (256, 128), 1)
    for pair in range(4):
        rows = pl.ds(256 * pair, 256)
        data = (high_ref[rows, :], low_ref[rows, :])

        def mixed(kind):
            return product((mats_ref[kind, 0], mats_ref[kind, 1]), data, ((1,), (1,)))

        low_half, high_half = mixed(POS), mixed(NEG)
        if pair == 0:
            zero, half = mixed(ZERO), mixed(HALF)
        for side in range(2):
            at = slice(128 * side, 128 * side + 128)
            block = jnp.where(lane < 64, low_half[:, at], high_half[:, at])
            if pair == 0 and side == 0:
                block = jnp.where(lane < 32, zero[:, at], block)
                block = jnp.where((lane >= 64) & (lane < 96), half[:, at], block)
            out_ref[pl.ds(64 * pair + 32 * side, 32)] = block.reshape(32, 8, 128)


def sine_turns(turns):
    t = turns - jnp.round(turns)
    square = t * t
    total = SINE[-1]
    for coefficient in SINE[-2::-1]:
        total = total * square + coefficient
    return total * t


def sine_fit():
    nodes = np.cos(np.pi * (np.arange(400) + 0.5) / 800) * 0.5
    basis = np.stack([nodes ** (2 * k + 1) for k in range(8)], 1)
    return [float(c) for c in np.linalg.lstsq(basis, np.sin(2 * np.pi * nodes), rcond=None)[0]]


SINE = sine_fit()


def device_number():
    return 8 * lax.axis_index("row") + lax.axis_index("col")


def columns_kernel(
    params_ref, field_ref, forward_ref, inverse_ref, ahead_ref, behind_ref, out_ref, work_ref, back_ref
):
    device = device_number()
    quad, group = device // 32, device % 32
    sub = lax.broadcasted_iota(jnp.int32, (8, 128), 0)
    lane = lax.broadcasted_iota(jnp.int32, (8, 128), 1)
    first = (sub & 2) == 0
    sign = jnp.where(first, 1.0, -1.0).astype(F32)
    side = jnp.where(lane < 64, 1.0, -1.0).astype(F32)

    def shift(value, amount, axis):
        return pltpu.roll(value, amount, axis + value.ndim - 2)

    def swap_pairs(value):
        return jnp.where(first, shift(value, 6, 0), shift(value, 2, 0))

    for nb in range(8):
        lines = []
        for na in range(16):
            n = 8 * na + nb
            one, two = field_ref[2 * n], field_ref[2 * n + 1]
            lines.append(
                (jnp.where(first, one, shift(two, 2, 0)), jnp.where(first, shift(one, 6, 0), two))
            )
        for ka, line in enumerate(transform(lines, -1)):
            real, imag = turned(line, nb * ka, 128, -1)
            work_ref[0, ka, nb] = real
            work_ref[1, ka, nb] = imag

    slot = lane >> 5
    s = ((sub >> 2) << 1) | (sub & 1)
    positive = 4 * group + s
    base = 2 * group + (s & 1)
    mirrored = jnp.where(s < 2, base, jnp.where(base == 0, 64, 128 - base))
    halfway = jnp.where(s < 2, base, 127 - base)
    k2 = jnp.where(slot < 2, positive, 127 - positive)
    k1 = 2 * quad + (slot & 1)
    k1 = jnp.where(slot < 2, k1, 32 - k1)
    special = (quad == 0) & ((slot & 1) == 0)
    k2 = jnp.where(special, jnp.where(slot == 0, mirrored, halfway), k2)
    k1 = jnp.where(special, jnp.where(slot == 0, 0, 16), k1)
    v = k1 + 32 * k2
    v = jnp.where(v >= N // 2, v - N, v).astype(F32)
    v_square = v * v
    a2 = lane & 15
    u_base = (64 * (sub & 2) + 256 * a2 - jnp.where(a2 >= 8, N, 0)).astype(F32)
    later = (lane & 16) != 0
    rate_even = jnp.where(later, params_ref[2], params_ref[0])
    rate_odd = jnp.where(later, params_ref[3], params_ref[1])
    offset, gain, floor = params_ref[4], params_ref[5], params_ref[6]

    def rows_of(table, which, start, count, stride):
        picked = []
        for part in range(2):
            tiles = []
            for k in range(count):
                at = pl.ds(start + stride * k, 1)
                upper = jnp.broadcast_to(table[which + (part, 0, at)], (8, 128))
                lower = jnp.broadcast_to(table[which + (part, 1, at)], (8, 128))
                tiles.append(jnp.where(first, upper, lower))
            picked.append(jnp.stack(tiles))
        return picked

    forward = (forward_ref[0], forward_ref[1])
    inverse = (inverse_ref[0], inverse_ref[1])
    natural = ((1,), (0,))
    for bunch in range(4):
        reals, imags = [], []
        for ka in range(4 * bunch, 4 * bunch + 4):
            lines = transform([(work_ref[0, ka, nb], work_ref[1, ka, nb]) for nb in range(8)], -1)
            turned_lines = []
            for kb, line in enumerate(lines):
                angle = 2.0 * math.pi * (ka + 16 * kb) / 256
                line = times(
                    line,
                    jnp.where(first, 1.0, math.cos(angle)).astype(F32),
                    jnp.where(first, 0.0, -math.sin(angle)).astype(F32),
                )
                turned_lines.append(tuple(swap_pairs(z) + sign * z for z in line))
            real = jnp.stack([z[0] for z in turned_lines])
            imag = jnp.stack([z[1] for z in turned_lines])
            cosine, sine = rows_of(ahead_ref, (), ka, 8, 16)
            real, imag = times((real, imag), cosine, -sine)
            reals.append(real.reshape(64, 128))
            imags.append(imag.reshape(64, 128))
        mixed = jnp.concatenate(
            [jnp.concatenate(reals, 0), jnp.concatenate(imags, 0)], 1
        )
        mixed = product(split(mixed), forward, natural)
        reals, imags = [], []
        for step in range(4):
            ka = 4 * bunch + step
            rows = slice(64 * step, 64 * step + 64)
            real = mixed[rows, :128].reshape(8, 8, 128)
            imag = mixed[rows, 128:].reshape(8, 8, 128)
            w1 = ka + 16 * lax.broadcasted_iota(jnp.int32, (8, 8, 128), 0)
            u = u_base + w1.astype(F32)
            radius = u * u + v_square
            even = gain * sine_turns(radius * rate_even + offset)
            odd = gain * sine_turns(radius * rate_odd + offset)
            energy = even * even + odd * odd
            other = jnp.where(later, shift(energy, 16, 1), shift(energy, 112, 1))
            scale = 1.0 / (energy + other + floor)
            reals.append(((even * real + odd * imag) * scale).reshape(64, 128))
            imags.append(((even * imag - odd * real) * scale).reshape(64, 128))
        mixed = jnp.concatenate(
            [jnp.concatenate(reals, 0), jnp.concatenate(imags, 0)], 1
        )
        mixed = product(split(mixed), inverse, natural)
        for step in range(4):
            ka = 4 * bunch + step
            rows = slice(64 * step, 64 * step + 64)
            real = mixed[rows, :128].reshape(8, 8, 128)
            imag = mixed[rows, 128:].reshape(8, 8, 128)
            real = jnp.where(lane < 64, real[:4], real[4:])
            imag = jnp.where(lane < 64, imag[:4], imag[4:])
            cosine, sine = rows_of(behind_ref, (0,), ka, 4, 16)
            real, imag = times((real, imag), cosine, sine)
            real, imag = (swap_pairs(z) + sign * z for z in (real, imag))
            corner = (lane >= 64) & jnp.logical_not(first)
            real, imag = jnp.where(corner, -imag, real), jnp.where(corner, real, imag)
            real, imag = (shift(z, 64, 1) + side * z for z in (real, imag))
            cosine, sine = rows_of(behind_ref, (1,), ka, 4, 16)
            real, imag = times((real, imag), cosine, sine)
            back_ref[0, ka] = real
            back_ref[1, ka] = imag

    for wb in range(8):
        lines = [
            tuple(back_ref[part, wb + 8 * (wa % 2), wa // 2] for part in range(2)) for wa in range(8)
        ]
        for na, line in enumerate(transform(lines, 1)):
            real, imag = turned(line, wb * na, 64, 1)
            work_ref[0, na, wb] = real
            work_ref[1, na, wb] = imag
    bit5 = (lane & 32) != 0
    reflected = (quad == 0) & ((lane & 16) == 0)
    itself = (quad == 0) & (group == 0) & ((lane & 48) == 0) & ((sub & 1) == 0)
    low_half = (lane & 8) == 0
    straight = ((sub & 4) != 0) == (lane >= 64)

    def partner(value):
        across = jnp.where(bit5, shift(value, 32, 1), shift(value, 96, 1))
        down = jnp.where(itself, value, shift(value, 4, 0))
        return jnp.where(reflected, down, across)

    for na in range(8):
        lines = [(work_ref[0, na, wb], work_ref[1, na, wb]) for wb in range(8)]
        for nb, (real, imag) in enumerate(transform(lines, 1)):
            real, imag = real + partner(real), imag - partner(imag)
            packed = real + jnp.where(low_half, -shift(imag, 120, 1), shift(imag, 8, 1))
            crossed = shift(shift(packed, 64, 1), 4, 0)
            out_ref[na + 8 * nb] = jnp.where(straight, packed, crossed)


def image_kernel(field_ref, mats_ref, twist_ref, last_ref, out_ref):
    lane = lax.broadcasted_iota(jnp.int32, (64, 128), 1)
    bit6, bit3 = (lane & 64) != 0, (lane & 8) != 0
    blocks = []
    for pair in range(2):
        tiles = [field_ref[pl.ds(256 * pair + 64 * q, 64), :] for q in range(4)]
        parts = []
        for qb in range(2):
            one, two = tiles[qb], tiles[2 + qb]
            parts.append(
                (
                    jnp.where(bit6, pltpu.roll(two, 64, 1), one),
                    jnp.where(bit6, two, pltpu.roll(one, 64, 1)),
                )
            )
        stacked = []
        for s1 in range(2):
            one, two = parts[0][s1], parts[1][s1]
            stacked.append(jnp.where(bit3, pltpu.roll(two, 8, 1), one))
            stacked.append(jnp.where(bit3, two, pltpu.roll(one, 120, 1)))
        blocks.append(jnp.concatenate(stacked, 0))
    data = split(jnp.concatenate(blocks, 1))

    def mixed(kind):
        return product((mats_ref[kind, 0], mats_ref[kind, 1]), data, ((1,), (0,)))

    lane = lax.broadcasted_iota(jnp.int32, (256, 256), 1)
    value = jnp.where((lane & 32) == 0, mixed(POS), mixed(NEG))
    value = jnp.where((lane & (128 + 64 + 32 + 16 + 8)) == 0, mixed(ZERO), value)
    value = jnp.where((lane & (128 + 64 + 32 + 16 + 8)) == 32, mixed(HALF), value)
    real, imag = times((value[:128], value[128:]), twist_ref[0], twist_ref[1])
    lines = split(jnp.concatenate([real, imag], 1))
    image = product((last_ref[0], last_ref[1]), lines, ((1,), (1,)))
    for n1 in range(32):
        out_ref[n1 // 4, :, pl.ds(128 * (n1 % 4), 128)] = image[16 * n1 : 16 * n1 + 16]


def call(kernel, out_shape, scratch, arguments, scalars=0):
    in_specs = [
        pl.BlockSpec(memory_space=pltpu.SMEM if k < scalars else pltpu.VMEM)
        for k in range(len(arguments))
    ]
    return pl.pallas_call(
        kernel,
        out_shape=jax.ShapeDtypeStruct(out_shape, F32),
        in_specs=in_specs,
        out_specs=pl.BlockSpec(memory_space=pltpu.VMEM),
        scratch_shapes=scratch,
        compiler_params=pltpu.CompilerParams(vmem_limit_bytes=40 * 1024 * 1024),
    )(*arguments)


def image_rows(field):
    mats, twist = row_constants()
    scratch = [pltpu.VMEM((1024, 256), BF16), pltpu.VMEM((1024, 256), BF16)]
    return call(rows_kernel, (256, 8, 128), scratch, [field, jnp.asarray(mats), jnp.asarray(twist)])


def filter_columns(field, fresnel, ctf_terms):
    ratio, regular = ctf_terms[0], ctf_terms[1]
    params = jnp.concatenate(
        [
            1.0 / (2.0 * N * N * fresnel),
            jnp.stack(
                [
                    jnp.arctan(ratio) * (0.5 / math.pi),
                    2.0 * jnp.sqrt(1.0 + ratio * ratio),
                    regular,
                    regular,
                ]
            ),
        ]
    )
    constants = [jnp.asarray(c) for c in column_constants()]
    scratch = [pltpu.VMEM((2, 16, 8, 8, 128), F32), pltpu.VMEM((2, 16, 4, 8, 128), F32)]
    return call(columns_kernel, (64, 8, 128), scratch, [params, field] + constants, scalars=1)


def image_from(field):
    constants = [jnp.asarray(c) for c in image_constants()]
    return call(image_kernel, (8, 16, 512), [], [field] + constants)


def exchange(field, axes):
    return lax.all_to_all(field, axes, split_axis=0, concat_axis=0, tiled=True)


def local(holograms, fresnel, ctf_terms):
    field = holograms.reshape(4, 8, 16, 512).transpose(1, 0, 2, 3)
    field = image_rows(exchange(field, "col"))
    field = filter_columns(exchange(field, ("row", "col")), fresnel, ctf_terms)
    field = exchange(field.reshape(256, 2, 128), ("row", "col"))
    image = image_from(field.reshape(512, 128))
    return exchange(image, "col").reshape(128, 512)


def solution(mesh):
    in_specs = (P(None, "row", "col"), P(), P())
    out_specs = P("row", "col")
    return jax.shard_map(local, mesh=mesh, in_specs=in_specs, out_specs=out_specs, check_vma=False)
```

profile of v0, /device:TPU:1, one launch (start us, length us, event | category | flops | bytes accessed | tf_op | source)
XLA Modules:
  0.0 108.1 jit_solution(4859213229582710222)
XLA Ops:
  0.0 1.3 %copy.15 = f32[4,8,16,512]{3,2,0,1:T(8,128)S(1)} copy(f32[4,8,16,512]{3,2,1,0:T(8,128)} %bitcast.10) | data formatting | bytes 2097152 | tf_op jit(solution)/shard_map/reshape | solution.py:481
  1.3 0.0 copy-start
  1.3 0.0 copy-start.8
  1.4 20.4 %all_to_all.20.field_ref = f32[8,4,16,512]{3,2,1,0:T(8,128)S(1)} all-to-all(f32[8,4,16,512]{3,2,1,0:T(8,128)S(1)} %bitcast.9), channel_id=1, replica_groups=mesh['row'=32,'col'=8] {'col'}, dimensions={0} | all-to-all | bytes 2097152 | tf_op jit(solution)/shard_map/all_to_all | solution.py:477
  21.8 0.0 copy-done
  21.8 0.0 copy-done.8
  21.8 2.5 %shard_map.118 = f32[256,8,128]{2,1,0:T(8,128)} custom-call(f32[8,4,16,512]{3,2,1,0:T(8,128)S(1)} %all_to_all.20.field_ref, bf16[4,2,256,256]{3,2,1,0:T(8,128)(2,1)S(1)} %copy-done, f32[2,32,128]{2,1,0:T(8,128)S(1)} %copy-done.8), custom_call_target="tpu_custom_call" | custom-call | tf_op jit(solution)/shard_map/pallas_call | solution.py:435
  24.3 0.0 copy-start.9
  24.3 0.0 copy-start.3
  24.3 13.6 %all-to-all-start.1 = ((f32[256,8,128]{2,1,0:T(8,128)}), f32[256,8,128]{2,1,0:T(8,128)S(1)}, u32[]{:S(2)}, u32[]{:S(2)}) async-start(f32[256,8,128]{2,1,0:T(8,128)} %shard_map.118), calls=%async_computation.1 | async-start | bytes 2097152 | tf_op jit(solution)/shard_map/all_to_all | solution.py:477
  37.9 0.0 copy-done.9
  37.9 0.6 fusion
  40.3 0.0 copy-start.10
  40.3 0.6 copy-done.10
  40.9 1.4 %concatenate.3.params_ref = f32[8]{0:T(128)S(1)} concatenate(f32[4]{0:T(128)S(1)} %multiply_divide_fusion, f32[1]{0:T(128)S(6)} %mul.12, f32[1]{0:T(128)S(6)} %mul_shard_map.4, f32[1]{0:T(128)} %get-tuple-element.5, f32[1]{0:T(128)} %get-tuple-element.5), dimensions={0} | concatenate | bytes 64 | tf_op jit(solution)/shard_map/concatenate | solution.py:453
  42.3 0.0 copy-start.1
  42.3 0.0 copy-start.2
  42.3 26.2 %all-to-all-done.1.field_ref = f32[256,8,128]{2,1,0:T(8,128)S(1)} async-done(((f32[256,8,128]{2,1,0:T(8,128)}), f32[256,8,128]{2,1,0:T(8,128)S(1)}, u32[]{:S(2)}, u32[]{:S(2)}) %all-to-all-start.1) | async-done | bytes 1048608 | tf_op jit(solution)/shard_map/all_to_all | solution.py:477
  68.5 0.0 copy-done.3
  68.5 0.0 copy-start.4
  68.5 0.9 copy-done.4
  69.5 0.0 copy-start.5
  69.5 0.9 copy-done.5
  70.4 0.0 copy-start.6
  70.4 0.9 copy-done.6
  71.4 4.0 %shard_map.119 = f32[64,8,128]{2,1,0:T(8,128)S(1)} custom-call(f32[8]{0:T(128)S(1)} %concatenate.3.params_ref, f32[256,8,128]{2,1,0:T(8,128)S(1)} %all-to-all-done.1.field_ref, bf16[2,256,256]{2,1,0:T(8,128)(2,1)S(1)} %copy-done.6, bf16[2,256,256]{2,1,0:T(8,128)(2,1)S(1)} %copy-done.5, f32[2,2,128,128]{3,2,1,0:T(8,128)S(1)} %copy-done.4, ...), custom_call_target="tpu_custom_call" | custom-call | tf_op jit(solution)/shard_map/pallas_call | solution.py:435
  75.4 0.0 copy-start.7
  75.4 22.2 %all_to_all.21 = f32[256,2,128]{2,1,0:T(2,128)S(1)} all-to-all(f32[256,2,128]{2,1,0:T(2,128)S(1)} %bitcast.7), channel_id=1, replica_groups=mesh['row'=32,'col'=8] {'row','col'}, dimensions={0} | all-to-all | bytes 524288 | tf_op jit(solution)/shard_map/all_to_all | solution.py:477
  97.6 0.0 copy-done.1
  97.6 0.0 copy-done.2
  97.6 0.0 copy-done.7
  97.6 1.3 %shard_map.120 = f32[8,16,512]{2,1,0:T(8,128)S(1)} custom-call(f32[512,128]{1,0:T(8,128)S(1)} %bitcast.8, bf16[4,2,256,256]{3,2,1,0:T(8,128)(2,1)S(1)} %copy-done.2, f32[2,128,256]{2,1,0:T(8,128)S(1)} %copy-done.7, bf16[2,512,512]{2,1,0:T(8,128)(2,1)S(1)} %copy-done.1), custom_call_target="tpu_custom_call" | custom-call | tf_op jit(solution)/shard_map/pallas_call | solution.py:435
  98.9 8.5 %all_to_all.22 = f32[8,16,512]{2,1,0:T(8,128)S(1)} all-to-all(f32[8,16,512]{2,1,0:T(8,128)S(1)} %shard_map.120), channel_id=1, replica_groups=mesh['row'=32,'col'=8] {'col'}, dimensions={0} | all-to-all | bytes 524288 | tf_op jit(solution)/shard_map/all_to_all | solution.py:477
  107.4 0.7 copy.17
  (1 shorter events, 0.0 us)
Async XLA Ops:
  1.3 20.5 %copy-start = (bf16[4,2,256,256]{3,2,1,0:T(8,128)(2,1)S(1)}, bf16[4,2,256,256]{3,2,1,0:T(8,128)(2,1)}, u32[]{:S(2)}) copy-start(bf16[4,2,256,256]{3,2,1,0:T(8,128)(2,1)} %constant.32.clone.mats_ref) | copy-start | bytes 3145732
  1.3 20.4 %copy-start.8 = (f32[2,32,128]{2,1,0:T(8,128)S(1)}, f32[2,32,128]{2,1,0:T(8,128)}, u32[]{:S(2)}) copy-start(f32[2,32,128]{2,1,0:T(8,128)} %constant.33.clone.twist_ref) | copy-start | bytes 98308
  24.3 13.6 %copy-start.9 = (f32[2]{0:T(128)S(1)}, f32[2]{0:T(128)}, u32[]{:S(2)}) copy-start(f32[2]{0:T(128)} %param.14) | copy-start | bytes 28
  24.3 44.3 %copy-start.3 = (f32[2,2,2,64,128]{4,3,2,1,0:T(8,128)S(1)}, f32[2,2,2,64,128]{4,3,2,1,0:T(8,128)}, u32[]{:S(2)}) copy-start(f32[2,2,2,64,128]{4,3,2,1,0:T(8,128)} %constant.37.clone.behind_ref) | copy-start | bytes 786436
  24.3 44.3 %all-to-all-start.1 = ((f32[256,8,128]{2,1,0:T(8,128)}), f32[256,8,128]{2,1,0:T(8,128)S(1)}, u32[]{:S(2)}, u32[]{:S(2)}) async-start(f32[256,8,128]{2,1,0:T(8,128)} %shard_map.118), calls=%async_computation.1 | async-start | bytes 2097152 | tf_op jit(solution)/shard_map/all_to_all | solution.py:477
  40.3 0.7 copy-start.10
  42.3 55.3 %copy-start.1 = (bf16[2,512,512]{2,1,0:T(8,128)(2,1)S(1)}, bf16[2,512,512]{2,1,0:T(8,128)(2,1)}, u32[]{:S(2)}) copy-start(bf16[2,512,512]{2,1,0:T(8,128)(2,1)} %constant.40.clone.last_ref) | copy-start | bytes 3145732
  42.3 55.3 %copy-start.2 = (bf16[4,2,256,256]{3,2,1,0:T(8,128)(2,1)S(1)}, bf16[4,2,256,256]{3,2,1,0:T(8,128)(2,1)}, u32[]{:S(2)}) copy-start(bf16[4,2,256,256]{3,2,1,0:T(8,128)(2,1)} %constant.38.clone.mats_ref) | copy-start | bytes 3145732
  68.5 1.0 copy-start.4
  69.5 0.9 copy-start.5
  70.4 0.9 copy-start.6
  75.4 22.2 %copy-start.7 = (f32[2,128,256]{2,1,0:T(8,128)S(1)}, f32[2,128,256]{2,1,0:T(8,128)}, u32[]{:S(2)}) copy-start(f32[2,128,256]{2,1,0:T(8,128)} %constant.39.clone.twist_ref) | copy-start | bytes 786436
where the time goes:
time: 109 us; the launch traced here: 108 us
  blocking collectives  51.1 us (47%)
  waiting for transfers between devices  26.2 us (24%)
  starting transfers between devices  13.6 us (12%)
  Pallas kernels  7.77 us (7%)
  local copies, waits for them, and re-layouts  7.52 us (7%)
  between operations  1.9 us (2%)
    all_to_all x3, blocking collectives, exchange(): return lax.all_to_all(field, axes, split_axis=0, concat_axis=0, tiled=True)  51.1 us
    all_to_all x1, waiting for transfers between devices, exchange(): return lax.all_to_all(field, axes, split_axis=0, concat_axis=0, tiled=True)  26.2 us
    all_to_all x1, starting transfers between devices, exchange(): return lax.all_to_all(field, axes, split_axis=0, concat_axis=0, tiled=True)  13.6 us
    pallas_call x3, Pallas kernels, call(): pl.pallas_call(kernel, out_shape=jax.ShapeDtypeStruct(out_shape, F32), in...  7.77 us
    unnamed x23, local copies, waits for them, and re-layouts  4.24 us
  transfers between devices with their start and end apart: 1, of which 1 were waited for; matrix products, arithmetic and copies ran while one was open for 2% of the time, Pallas kernels for 0%

commit v1 on v0

--- a/solution.py
+++ b/solution.py
@@ -81,7 +81,7 @@
     behind = np.stack(turn(step * within, N)).astype(np.float32)
     step = np.arange(2)[:, None, None] + 2 * top
     spin = np.stack(turn(step * np.arange(64)[None, :, None], 256)).astype(np.float32)
-    return halves(forward), halves(inverse), ahead, np.stack([behind, spin])
+    return np.concatenate([halves(forward), halves(inverse)]), ahead, np.stack([behind, spin])
 
 
 def image_constants():
@@ -234,9 +234,39 @@
     return 8 * lax.axis_index("row") + lax.axis_index("col")
 
 
+def arc_tangent(value):
+    for _ in range(2):
+        value = value / (1.0 + jnp.sqrt(1.0 + value * value))
+    square = value * value
+    total = 1.0 / 17.0
+    for k in range(15, 0, -2):
+        total = 1.0 / k - square * total
+    return 4.0 * value * total
+
+
 def columns_kernel(
-    params_ref, field_ref, forward_ref, inverse_ref, ahead_ref, behind_ref, out_ref, work_ref, back_ref
+    fresnel_ref,
+    terms_ref,
+    field_ref,
+    mats_hbm,
+    ahead_hbm,
+    behind_hbm,
+    out_ref,
+    work_ref,
+    back_ref,
+    mats_ref,
+    ahead_ref,
+    behind_ref,
+    sems,
 ):
+    copies = [
+        pltpu.make_async_copy(source, target, sems.at[k])
+        for k, (source, target) in enumerate(
+            [(mats_hbm, mats_ref), (ahead_hbm, ahead_ref), (behind_hbm, behind_ref)]
+        )
+    ]
+    for copy in copies:
+        copy.start()
     device = device_number()
     quad, group = device // 32, device % 32
     sub = lax.broadcasted_iota(jnp.int32, (8, 128), 0)
@@ -282,9 +312,12 @@
     a2 = lane & 15
     u_base = (64 * (sub & 2) + 256 * a2 - jnp.where(a2 >= 8, N, 0)).astype(F32)
     later = (lane & 16) != 0
-    rate_even = jnp.where(later, params_ref[2], params_ref[0])
-    rate_odd = jnp.where(later, params_ref[3], params_ref[1])
-    offset, gain, floor = params_ref[4], params_ref[5], params_ref[6]
+    rate_even = (0.5 / (N * N)) / jnp.where(later, fresnel_ref[2], fresnel_ref[0])
+    rate_odd = (0.5 / (N * N)) / jnp.where(later, fresnel_ref[3], fresnel_ref[1])
+    ratio = jnp.full((8, 128), terms_ref[0], F32)
+    offset = arc_tangent(ratio) * (0.5 / math.pi)
+    gain = 2.0 * jnp.sqrt(1.0 + ratio * ratio)
+    floor = terms_ref[1]
 
     def rows_of(table, which, start, count, stride):
         picked = []
@@ -298,8 +331,10 @@
             picked.append(jnp.stack(tiles))
         return picked
 
-    forward = (forward_ref[0], forward_ref[1])
-    inverse = (inverse_ref[0], inverse_ref[1])
+    for copy in copies:
+        copy.wait()
+    forward = (mats_ref[0], mats_ref[1])
+    inverse = (mats_ref[2], mats_ref[3])
     natural = ((1,), (0,))
     for bunch in range(4):
         reals, imags = [], []
@@ -427,15 +462,11 @@
         out_ref[n1 // 4, :, pl.ds(128 * (n1 % 4), 128)] = image[16 * n1 : 16 * n1 + 16]
 
 
-def call(kernel, out_shape, scratch, arguments, scalars=0):
-    in_specs = [
-        pl.BlockSpec(memory_space=pltpu.SMEM if k < scalars else pltpu.VMEM)
-        for k in range(len(arguments))
-    ]
+def call(kernel, out_shape, scratch, arguments, spaces):
     return pl.pallas_call(
         kernel,
         out_shape=jax.ShapeDtypeStruct(out_shape, F32),
-        in_specs=in_specs,
+        in_specs=[pl.BlockSpec(memory_space=space) for space in spaces],
         out_specs=pl.BlockSpec(memory_space=pltpu.VMEM),
         scratch_shapes=scratch,
         compiler_params=pltpu.CompilerParams(vmem_limit_bytes=40 * 1024 * 1024),
@@ -443,34 +474,23 @@
 
 
 def image_rows(field):
-    mats, twist = row_constants()
+    arguments = [field] + [jnp.asarray(c) for c in row_constants()]
     scratch = [pltpu.VMEM((1024, 256), BF16), pltpu.VMEM((1024, 256), BF16)]
-    return call(rows_kernel, (256, 8, 128), scratch, [field, jnp.asarray(mats), jnp.asarray(twist)])
+    return call(rows_kernel, (256, 8, 128), scratch, arguments, [pltpu.VMEM] * 3)
 
 
 def filter_columns(field, fresnel, ctf_terms):
-    ratio, regular = ctf_terms[0], ctf_terms[1]
-    params = jnp.concatenate(
-        [
-            1.0 / (2.0 * N * N * fresnel),
-            jnp.stack(
-                [
-                    jnp.arctan(ratio) * (0.5 / math.pi),
-                    2.0 * jnp.sqrt(1.0 + ratio * ratio),
-                    regular,
-                    regular,
-                ]
-            ),
-        ]
-    )
     constants = [jnp.asarray(c) for c in column_constants()]
     scratch = [pltpu.VMEM((2, 16, 8, 8, 128), F32), pltpu.VMEM((2, 16, 4, 8, 128), F32)]
-    return call(columns_kernel, (64, 8, 128), scratch, [params, field] + constants, scalars=1)
+    scratch += [pltpu.VMEM(c.shape, c.dtype) for c in constants] + [pltpu.SemaphoreType.DMA((3,))]
+    spaces = [pltpu.SMEM] * 2 + [pltpu.VMEM] + [pltpu.HBM] * 3
+    arguments = [fresnel, ctf_terms, field] + constants
+    return call(columns_kernel, (64, 8, 128), scratch, arguments, spaces)
 
 
 def image_from(field):
-    constants = [jnp.asarray(c) for c in image_constants()]
-    return call(image_kernel, (8, 16, 512), [], [field] + constants)
+    arguments = [field] + [jnp.asarray(c) for c in image_constants()]
+    return call(image_kernel, (8, 16, 512), [], arguments, [pltpu.VMEM] * 4)
 
 
 def exchange(field, axes):

time: 109 us -> 105 us (0.963)
  blocking collectives: 51.1 us -> 95.2 us
  waiting for transfers between devices: 26.2 us -> 0 us
  starting transfers between devices: 13.6 us -> 0 us
  local copies, waits for them, and re-layouts: 7.52 us -> 2.09 us
  between operations: 1.9 us -> 0.14 us
    all_to_all x3 -> x4, blocking collectives: 51.1 us -> 95.2 us  [exchange(): return lax.all_to_all(field, axes, split_axis=0, concat_axis=0, tiled=True)]
    all_to_all x1 -> x0, waiting for transfers between devices: 26.2 us -> none  [exchange(): return lax.all_to_all(field, axes, split_axis=0, concat_axis=0, tiled=True)]
    all_to_all x1 -> x0, starting transfers between devices: 13.6 us -> none  [exchange(): return lax.all_to_all(field, axes, split_axis=0, concat_axis=0, tiled=True)]
    unnamed x23 -> x21, local copies, waits for them, and re-layouts: 4.24 us -> 0.77 us
    concatenate x1 -> x0, local copies, waits for them, and re-layouts: 1.38 us -> none  [filter_columns(): jnp.concatenate([1.0 / (2.0 * N * N * fresnel), jnp.stack([jnp.arctan(rat...]
  transfers between devices with their start and end apart: 1 -> 0, of which waited for: 1 -> 0; matrix products, arithmetic and copies ran while one was open for 2% -> 0% of each run, Pallas kernels for 0% -> 0%
where the time goes in v1:
time: 105 us; the launch traced here: 104 us
  blocking collectives  95.2 us (91%)
  Pallas kernels  7 us (7%)
  local copies, waits for them, and re-layouts  2.09 us (2%)
    all_to_all x4, blocking collectives, exchange(): return lax.all_to_all(field, axes, split_axis=0, concat_axis=0, tiled=True)  95.2 us
    pallas_call x3, Pallas kernels, call(): pl.pallas_call(kernel, out_shape=jax.ShapeDtypeStruct(out_shape, F32), in...  7 us

profile of v1, /device:TPU:1, one launch (start us, length us, event | category | flops | bytes accessed | tf_op | source)
XLA Modules:
  0.0 104.4 jit_solution(4434605598414714506)
XLA Ops:
  0.0 1.3 %copy.14 = f32[4,8,16,512]{3,2,0,1:T(8,128)S(1)} copy(f32[4,8,16,512]{3,2,1,0:T(8,128)} %bitcast.10) | data formatting | bytes 2097152 | tf_op jit(solution)/shard_map/reshape | solution.py:501
  1.3 0.0 copy-start
  1.3 0.0 copy-start.7
  1.4 20.4 %all_to_all.20.field_ref = f32[8,4,16,512]{3,2,1,0:T(8,128)S(1)} all-to-all(f32[8,4,16,512]{3,2,1,0:T(8,128)S(1)} %bitcast.9), channel_id=1, replica_groups=mesh['row'=32,'col'=8] {'col'}, dimensions={0} | all-to-all | bytes 2097152 | tf_op jit(solution)/shard_map/all_to_all | solution.py:497
  21.8 0.0 copy-done
  21.8 0.0 copy-done.7
  21.8 1.5 %shard_map.109 = f32[256,8,128]{2,1,0:T(8,128)S(1)} custom-call(f32[8,4,16,512]{3,2,1,0:T(8,128)S(1)} %all_to_all.20.field_ref, bf16[4,2,256,256]{3,2,1,0:T(8,128)(2,1)S(1)} %copy-done, f32[2,32,128]{2,1,0:T(8,128)S(1)} %copy-done.7), custom_call_target="tpu_custom_call" | custom-call | tf_op jit(solution)/shard_map/pallas_call | solution.py:466
  23.3 0.0 copy-start.3
  23.3 0.0 copy-start.4
  23.3 0.0 copy-start.5
  23.3 0.0 copy-start.8
  23.3 0.0 copy-start.9
  23.4 44.1 %all_to_all.21.field_ref = f32[256,8,128]{2,1,0:T(8,128)S(1)} all-to-all(f32[256,8,128]{2,1,0:T(8,128)S(1)} %shard_map.109), channel_id=1, replica_groups=mesh['row'=32,'col'=8] {'row','col'}, dimensions={0} | all-to-all | bytes 2097152 | tf_op jit(solution)/shard_map/all_to_all | solution.py:497
  67.4 0.0 copy-done.3
  67.4 0.0 copy-done.4
  67.4 0.0 copy-done.5
  67.4 0.0 copy-done.8
  67.4 0.0 copy-done.9
  67.5 0.0 copy-start.1
  67.5 0.0 copy-start.2
  67.5 4.2 %shard_map.110 = f32[64,8,128]{2,1,0:T(8,128)S(1)} custom-call(f32[4]{0:T(128)S(1)} %copy-done.8, f32[2]{0:T(128)S(1)} %copy-done.9, f32[256,8,128]{2,1,0:T(8,128)S(1)} %all_to_all.21.field_ref, bf16[4,256,256]{2,1,0:T(8,128)(2,1)S(1)} %copy-done.3, f32[2,2,128,128]{3,2,1,0:T(8,128)S(1)} %copy-done.5, f32[2,2,2,64,128]{4,3,2,1,0:T(8,128)S(1)} %copy-done.4), custom_call_target="tpu_custom_call" | custom-call | tf_op jit(solution)/shard_map/pallas_call | solution.py:466
  71.7 0.0 copy-start.6
  71.7 22.2 %all_to_all.22 = f32[256,2,128]{2,1,0:T(2,128)S(1)} all-to-all(f32[256,2,128]{2,1,0:T(2,128)S(1)} %bitcast.7), channel_id=1, replica_groups=mesh['row'=32,'col'=8] {'row','col'}, dimensions={0} | all-to-all | bytes 524288 | tf_op jit(solution)/shard_map/all_to_all | solution.py:497
  93.9 0.0 copy-done.1
  93.9 0.0 copy-done.2
  93.9 0.0 copy-done.6
  93.9 1.3 %shard_map.111 = f32[8,16,512]{2,1,0:T(8,128)S(1)} custom-call(f32[512,128]{1,0:T(8,128)S(1)} %bitcast.8, bf16[4,2,256,256]{3,2,1,0:T(8,128)(2,1)S(1)} %copy-done.2, f32[2,128,256]{2,1,0:T(8,128)S(1)} %copy-done.6, bf16[2,512,512]{2,1,0:T(8,128)(2,1)S(1)} %copy-done.1), custom_call_target="tpu_custom_call" | custom-call | tf_op jit(solution)/shard_map/pallas_call | solution.py:466
  95.2 8.5 %all_to_all.23 = f32[8,16,512]{2,1,0:T(8,128)S(1)} all-to-all(f32[8,16,512]{2,1,0:T(8,128)S(1)} %shard_map.111), channel_id=1, replica_groups=mesh['row'=32,'col'=8] {'col'}, dimensions={0} | all-to-all | bytes 524288 | tf_op jit(solution)/shard_map/all_to_all | solution.py:497
  103.7 0.7 copy.16
Async XLA Ops:
  1.3 20.5 %copy-start = (bf16[4,2,256,256]{3,2,1,0:T(8,128)(2,1)S(1)}, bf16[4,2,256,256]{3,2,1,0:T(8,128)(2,1)}, u32[]{:S(2)}) copy-start(bf16[4,2,256,256]{3,2,1,0:T(8,128)(2,1)} %constant.16.clone.mats_ref) | copy-start | bytes 3145732
  1.3 20.4 %copy-start.7 = (f32[2,32,128]{2,1,0:T(8,128)S(1)}, f32[2,32,128]{2,1,0:T(8,128)}, u32[]{:S(2)}) copy-start(f32[2,32,128]{2,1,0:T(8,128)} %constant.17.clone.twist_ref) | copy-start | bytes 98308
  23.3 44.1 %copy-start.3 = (bf16[4,256,256]{2,1,0:T(8,128)(2,1)S(1)}, bf16[4,256,256]{2,1,0:T(8,128)(2,1)}, u32[]{:S(2)}) copy-start(bf16[4,256,256]{2,1,0:T(8,128)(2,1)} %constant.18.clone.mats_hbm) | copy-start | bytes 1572868
  23.3 44.1 %copy-start.4 = (f32[2,2,2,64,128]{4,3,2,1,0:T(8,128)S(1)}, f32[2,2,2,64,128]{4,3,2,1,0:T(8,128)}, u32[]{:S(2)}) copy-start(f32[2,2,2,64,128]{4,3,2,1,0:T(8,128)} %constant.20.clone.behind_hbm) | copy-start | bytes 786436
  23.3 44.1 %copy-start.5 = (f32[2,2,128,128]{3,2,1,0:T(8,128)S(1)}, f32[2,2,128,128]{3,2,1,0:T(8,128)}, u32[]{:S(2)}) copy-start(f32[2,2,128,128]{3,2,1,0:T(8,128)} %constant.19.clone.ahead_hbm) | copy-start | bytes 786436
  23.3 44.1 %copy-start.8 = (f32[4]{0:T(128)S(1)}, f32[4]{0:T(128)}, u32[]{:S(2)}) copy-start(f32[4]{0:T(128)} %fresnel_ref.1) | copy-start | bytes 52
  23.3 44.1 %copy-start.9 = (f32[2]{0:T(128)S(1)}, f32[2]{0:T(128)}, u32[]{:S(2)}) copy-start(f32[2]{0:T(128)} %terms_ref.1) | copy-start | bytes 28
  67.5 26.4 %copy-start.1 = (bf16[2,512,512]{2,1,0:T(8,128)(2,1)S(1)}, bf16[2,512,512]{2,1,0:T(8,128)(2,1)}, u32[]{:S(2)}) copy-start(bf16[2,512,512]{2,1,0:T(8,128)(2,1)} %constant.23.clone.last_ref) | copy-start | bytes 3145732
  67.5 26.4 %copy-start.2 = (bf16[4,2,256,256]{3,2,1,0:T(8,128)(2,1)S(1)}, bf16[4,2,256,256]{3,2,1,0:T(8,128)(2,1)}, u32[]{:S(2)}) copy-start(bf16[4,2,256,256]{3,2,1,0:T(8,128)(2,1)} %constant.21.clone.mats_ref) | copy-start | bytes 3145732
  71.7 22.2 %copy-start.6 = (f32[2,128,256]{2,1,0:T(8,128)S(1)}, f32[2,128,256]{2,1,0:T(8,128)}, u32[]{:S(2)}) copy-start(f32[2,128,256]{2,1,0:T(8,128)} %constant.22.clone.twist_ref) | copy-start | bytes 786436

commit v2 on v1

--- a/solution.py
+++ b/solution.py
@@ -19,6 +19,8 @@
     low, high = 2 * quad, 2 * quad + 1
     if quad == 0:
         return [0, 1, 16, 31]
+    if quad % 2:
+        return [32 - low, 32 - high, low, high]
     return [low, high, 32 - low, 32 - high]
 
 
@@ -41,6 +43,10 @@
 def turn(product, length):
     angle = 2.0 * np.pi * (np.asarray(product, np.int64) % length) / length
     return np.cos(angle), np.sin(angle)
+
+
+def line_twist():
+    return np.stack(turn(np.arange(32)[:, None] * np.arange(128), N)).astype(np.float32)
 
 
 def row_constants():
@@ -52,8 +58,7 @@
         imag = np.concatenate([-sine, cosine], -1)
         both = np.stack([real.reshape(32, 2, 2, 256), imag.reshape(32, 2, 2, 256)], 2)
         mats.append(halves(both.reshape(256, 256)))
-    twist = np.stack(turn(np.arange(32)[:, None] * np.arange(128), N)).astype(np.float32)
-    return np.stack(mats), twist
+    return np.stack(mats), line_twist()
 
 
 def column_constants():
@@ -89,20 +94,11 @@
     for kind in range(4):
         k2 = np.array([[member(kind, g, s) for g in range(32)] for s in range(4)])
         k2 = k2.reshape(2, 2, 32).transpose(0, 2, 1).reshape(2, 64)
-        cosine, sine = turn(np.arange(128)[:, None, None] * k2, 128)
-        real = np.stack([cosine, -sine], 2).reshape(128, 256)
-        imag = np.stack([sine, cosine], 2).reshape(128, 256)
-        mats.append(halves(np.concatenate([real, imag])))
-    lane = np.arange(256)
-    quad = 4 * (lane // 128) + 2 * (lane // 64 % 2) + lane // 8 % 2
-    k1 = np.array([residues(q)[s] for q, s in zip(quad, lane // 16 % 4)])
-    twist = np.stack(turn(np.arange(128)[:, None] * k1, N)).astype(np.float32)
-    cosine, sine = turn(np.arange(32)[:, None] * k1, 32)
-    same = (np.arange(8)[:, None] == lane % 8).astype(np.float64)
-    real = np.concatenate([cosine[:, None] * same, -sine[:, None] * same], -1)
-    imag = np.concatenate([sine[:, None] * same, cosine[:, None] * same], -1)
-    last = np.concatenate([real, imag], 1).reshape(512, 512) * (0.5 / (N * N))
-    return np.stack(mats), twist, halves(last)
+        cosine, sine = turn(k2[:, :, None] * np.arange(128), 128)
+        real = np.concatenate([cosine, sine], -1)
+        imag = np.concatenate([-sine, cosine], -1)
+        mats.append(halves(np.stack([real, imag], 1).reshape(256, 256) * (0.5 / (N * N))))
+    return np.stack(mats), line_twist()
 
 
 def turned(value, angle_index, length, sign):
@@ -182,34 +178,34 @@
                 (field_ref[n1 // 4, 2 * j, :, at], field_ref[n1 // 4, 2 * j + 1, :, at])
             )
         lines = transform(lines, -1)
-        for quad in range(8):
-            for slot, k1 in enumerate(residues(quad)):
-                line = lines[k1]
-                if k1:
-                    line = times(line, twist_ref[0, pl.ds(k1, 1), :], -twist_ref[1, pl.ds(k1, 1), :])
-                rows = pl.ds(128 * quad + 32 * slot + 16 * j, 16)
-                for part in range(2):
-                    high, low = split(line[part])
-                    high_ref[rows, pl.ds(128 * part, 128)] = high
-                    low_ref[rows, pl.ds(128 * part, 128)] = low
+        for k1, line in enumerate(lines):
+            if k1:
+                line = times(line, twist_ref[0, pl.ds(k1, 1), :], -twist_ref[1, pl.ds(k1, 1), :])
+            place = 32 * k1 if k1 < 16 else 512 + 32 * ((32 - k1) % 16 ^ 2)
+            rows = pl.ds(place + 16 * j, 16)
+            for part in range(2):
+                high, low = split(line[part])
+                high_ref[rows, pl.ds(128 * part, 128)] = high
+                low_ref[rows, pl.ds(128 * part, 128)] = low
+
+    def mixed(kind, start, count):
+        rows = pl.ds(start, count)
+        data = (high_ref[rows, :], low_ref[rows, :])
+        return product((mats_ref[kind, 0], mats_ref[kind, 1]), data, ((1,), (1,)))
+
     lane = lax.broadcasted_iota(jnp.int32, (256, 128), 1)
-    for pair in range(4):
-        rows = pl.ds(256 * pair, 256)
-        data = (high_ref[rows, :], low_ref[rows, :])
-
-        def mixed(kind):
-            return product((mats_ref[kind, 0], mats_ref[kind, 1]), data, ((1,), (1,)))
-
-        low_half, high_half = mixed(POS), mixed(NEG)
-        if pair == 0:
-            zero, half = mixed(ZERO), mixed(HALF)
-        for side in range(2):
-            at = slice(128 * side, 128 * side + 128)
-            block = jnp.where(lane < 64, low_half[:, at], high_half[:, at])
-            if pair == 0 and side == 0:
-                block = jnp.where(lane < 32, zero[:, at], block)
-                block = jnp.where((lane >= 64) & (lane < 96), half[:, at], block)
-            out_ref[pl.ds(64 * pair + 32 * side, 32)] = block.reshape(32, 8, 128)
+    for half in range(2):
+        positive, negative = mixed(POS, 256 * half, 256), mixed(NEG, 512 + 256 * half, 256)
+        for pair in range(2):
+            at = slice(128 * pair, 128 * pair + 128)
+            one, two = positive[:, at], negative[:, at]
+            even, odd = jnp.where(lane < 64, one, two), jnp.where(lane < 64, two, one)
+            if half == 0 and pair == 0:
+                even = jnp.where(lane < 32, mixed(ZERO, 0, 128), even)
+                even = jnp.where((lane & 96) == 64, mixed(HALF, 512, 128), even)
+            for side, block in enumerate([even, odd]):
+                quad = 4 * half + 2 * pair + side
+                out_ref[pl.ds(32 * quad, 32)] = block.reshape(32, 8, 128)
 
 
 def sine_turns(turns):
@@ -223,7 +219,7 @@
 
 def sine_fit():
     nodes = np.cos(np.pi * (np.arange(400) + 0.5) / 800) * 0.5
-    basis = np.stack([nodes ** (2 * k + 1) for k in range(8)], 1)
+    basis = np.stack([nodes ** (2 * k + 1) for k in range(6)], 1)
     return [float(c) for c in np.linalg.lstsq(basis, np.sin(2 * np.pi * nodes), rcond=None)[0]]
 
 
@@ -294,7 +290,7 @@
             work_ref[0, ka, nb] = real
             work_ref[1, ka, nb] = imag
 
-    slot = lane >> 5
+    slot = (lane >> 5) ^ (2 * (quad & 1))
     s = ((sub >> 2) << 1) | (sub & 1)
     positive = 4 * group + s
     base = 2 * group + (s & 1)
@@ -425,15 +421,15 @@
             out_ref[na + 8 * nb] = jnp.where(straight, packed, crossed)
 
 
-def image_kernel(field_ref, mats_ref, twist_ref, last_ref, out_ref):
+def image_kernel(field_ref, mats_ref, twist_ref, out_ref):
     lane = lax.broadcasted_iota(jnp.int32, (64, 128), 1)
     bit6, bit3 = (lane & 64) != 0, (lane & 8) != 0
-    blocks = []
-    for pair in range(2):
-        tiles = [field_ref[pl.ds(256 * pair + 64 * q, 64), :] for q in range(4)]
+    tiles = {}
+    for half in range(2):
+        quads = [field_ref[pl.ds(256 * half + 64 * q, 64), :] for q in range(4)]
         parts = []
         for qb in range(2):
-            one, two = tiles[qb], tiles[2 + qb]
+            one, two = quads[qb], quads[2 + qb]
             parts.append(
                 (
                     jnp.where(bit6, pltpu.roll(two, 64, 1), one),
@@ -445,21 +441,27 @@
             one, two = parts[0][s1], parts[1][s1]
             stacked.append(jnp.where(bit3, pltpu.roll(two, 8, 1), one))
             stacked.append(jnp.where(bit3, two, pltpu.roll(one, 120, 1)))
-        blocks.append(jnp.concatenate(stacked, 0))
-    data = split(jnp.concatenate(blocks, 1))
-
-    def mixed(kind):
-        return product((mats_ref[kind, 0], mats_ref[kind, 1]), data, ((1,), (0,)))
-
-    lane = lax.broadcasted_iota(jnp.int32, (256, 256), 1)
-    value = jnp.where((lane & 32) == 0, mixed(POS), mixed(NEG))
-    value = jnp.where((lane & (128 + 64 + 32 + 16 + 8)) == 0, mixed(ZERO), value)
-    value = jnp.where((lane & (128 + 64 + 32 + 16 + 8)) == 32, mixed(HALF), value)
-    real, imag = times((value[:128], value[128:]), twist_ref[0], twist_ref[1])
-    lines = split(jnp.concatenate([real, imag], 1))
-    image = product((last_ref[0], last_ref[1]), lines, ((1,), (1,)))
-    for n1 in range(32):
-        out_ref[n1 // 4, :, pl.ds(128 * (n1 % 4), 128)] = image[16 * n1 : 16 * n1 + 16]
+        lines = jnp.concatenate(stacked, 0).T
+        for q in range(4):
+            for slot, k1 in enumerate(residues(4 * half + q)):
+                start = 64 * (q // 2) + 16 * slot + 8 * (q % 2)
+                tiles[k1] = lines[start : start + 8]
+    lines = {}
+    for kind, members in (
+        (POS, [1, *range(1, 16)]),
+        (NEG, [17, *range(17, 32)]),
+        (ZERO, [0, 0]),
+        (HALF, [16, 16]),
+    ):
+        data = split(jnp.concatenate([tiles[k1] for k1 in members], 0))
+        value = product(data, (mats_ref[kind, 0], mats_ref[kind, 1]), ((1,), (0,)))
+        for k, k1 in enumerate(members):
+            line = (value[8 * k : 8 * k + 8, :128], value[8 * k : 8 * k + 8, 128:])
+            lines[k1] = times(line, twist_ref[0, pl.ds(k1, 1), :], twist_ref[1, pl.ds(k1, 1), :])
+    for n1, (real, imag) in enumerate(transform([lines[k1] for k1 in range(32)], 1)):
+        at = pl.ds(128 * (n1 % 4), 128)
+        out_ref[n1 // 4, pl.ds(0, 8), at] = real
+        out_ref[n1 // 4, pl.ds(8, 8), at] = imag
 
 
 def call(kernel, out_shape, scratch, arguments, spaces):
@@ -490,7 +492,7 @@
 
 def image_from(field):
     arguments = [field] + [jnp.asarray(c) for c in image_constants()]
-    return call(image_kernel, (8, 16, 512), [], arguments, [pltpu.VMEM] * 4)
+    return call(image_kernel, (8, 16, 512), [], arguments, [pltpu.VMEM] * 3)
 
 
 def exchange(field, axes):

time: 105 us -> 104 us (level)
  Pallas kernels: 7 us -> 5.9 us
    pallas_call x3, Pallas kernels: 7 us -> 5.9 us  [call(): pl.pallas_call(kernel, out_shape=jax.ShapeDtypeStruct(out_shape, F32), in...]
where the time goes in v2:
time: 104 us; the launch traced here: 103 us
  blocking collectives  95.2 us (92%)
  Pallas kernels  5.9 us (6%)
  local copies, waits for them, and re-layouts  2.08 us (2%)
    all_to_all x4, blocking collectives, exchange(): return lax.all_to_all(field, axes, split_axis=0, concat_axis=0, tiled=True)  95.2 us
    pallas_call x3, Pallas kernels, call(): pl.pallas_call(kernel, out_shape=jax.ShapeDtypeStruct(out_shape, F32), in...  5.9 us

profile of v2, /device:TPU:1, one launch (start us, length us, event | category | flops | bytes accessed | tf_op | source)
XLA Modules:
  0.0 103.3 jit_solution(4767826500148106531)
XLA Ops:
  0.0 1.3 %copy.13 = f32[4,8,16,512]{3,2,0,1:T(8,128)S(1)} copy(f32[4,8,16,512]{3,2,1,0:T(8,128)} %bitcast.10) | data formatting | bytes 2097152 | tf_op jit(solution)/shard_map/reshape | solution.py:503
  1.3 0.0 copy-start
  1.3 0.0 copy-start.5
  1.4 20.4 %all_to_all.20.field_ref = f32[8,4,16,512]{3,2,1,0:T(8,128)S(1)} all-to-all(f32[8,4,16,512]{3,2,1,0:T(8,128)S(1)} %bitcast.9), channel_id=1, replica_groups=mesh['row'=32,'col'=8] {'col'}, dimensions={0} | all-to-all | bytes 2097152 | tf_op jit(solution)/shard_map/all_to_all | solution.py:499
  21.8 0.0 copy-done
  21.8 0.0 copy-done.5
  21.8 1.2 %shard_map.100 = f32[256,8,128]{2,1,0:T(8,128)S(1)} custom-call(f32[8,4,16,512]{3,2,1,0:T(8,128)S(1)} %all_to_all.20.field_ref, bf16[4,2,256,256]{3,2,1,0:T(8,128)(2,1)S(1)} %copy-done, f32[2,32,128]{2,1,0:T(8,128)S(1)} %copy-done.5), custom_call_target="tpu_custom_call" | custom-call | tf_op jit(solution)/shard_map/pallas_call | solution.py:468
  23.0 0.0 copy-start.2
  23.0 0.0 copy-start.3
  23.0 0.0 copy-start.4
  23.1 0.0 copy-start.6
  23.1 0.0 copy-start.7
  23.1 44.1 %all_to_all.21.field_ref = f32[256,8,128]{2,1,0:T(8,128)S(1)} all-to-all(f32[256,8,128]{2,1,0:T(8,128)S(1)} %shard_map.100), channel_id=1, replica_groups=mesh['row'=32,'col'=8] {'row','col'}, dimensions={0} | all-to-all | bytes 2097152 | tf_op jit(solution)/shard_map/all_to_all | solution.py:499
  67.1 0.0 copy-done.2
  67.1 0.0 copy-done.3
  67.1 0.0 copy-done.4
  67.2 0.0 copy-done.6
  67.2 0.0 copy-done.7
  67.2 0.0 copy-start.1
  67.2 4.1 %shard_map.101 = f32[64,8,128]{2,1,0:T(8,128)S(1)} custom-call(f32[4]{0:T(128)S(1)} %copy-done.6, f32[2]{0:T(128)S(1)} %copy-done.7, f32[256,8,128]{2,1,0:T(8,128)S(1)} %all_to_all.21.field_ref, bf16[4,256,256]{2,1,0:T(8,128)(2,1)S(1)} %copy-done.2, f32[2,2,128,128]{3,2,1,0:T(8,128)S(1)} %copy-done.4, f32[2,2,2,64,128]{4,3,2,1,0:T(8,128)S(1)} %copy-done.3), custom_call_target="tpu_custom_call" | custom-call | tf_op jit(solution)/shard_map/pallas_call | solution.py:468
  71.3 22.2 %all_to_all.22 = f32[256,2,128]{2,1,0:T(2,128)S(1)} all-to-all(f32[256,2,128]{2,1,0:T(2,128)S(1)} %bitcast.7), channel_id=1, replica_groups=mesh['row'=32,'col'=8] {'row','col'}, dimensions={0} | all-to-all | bytes 524288 | tf_op jit(solution)/shard_map/all_to_all | solution.py:499
  93.4 0.0 copy-done.1
  93.4 0.6 shard_map.102
  94.0 8.5 %all_to_all.23 = f32[8,16,512]{2,1,0:T(8,128)S(1)} all-to-all(f32[8,16,512]{2,1,0:T(8,128)S(1)} %shard_map.102), channel_id=1, replica_groups=mesh['row'=32,'col'=8] {'col'}, dimensions={0} | all-to-all | bytes 524288 | tf_op jit(solution)/shard_map/all_to_all | solution.py:499
  102.6 0.7 copy.15
Async XLA Ops:
  1.3 20.5 %copy-start = (bf16[4,2,256,256]{3,2,1,0:T(8,128)(2,1)S(1)}, bf16[4,2,256,256]{3,2,1,0:T(8,128)(2,1)}, u32[]{:S(2)}) copy-start(bf16[4,2,256,256]{3,2,1,0:T(8,128)(2,1)} %constant.12.clone.mats_ref) | copy-start | bytes 3145732
  1.3 20.4 %copy-start.5 = (f32[2,32,128]{2,1,0:T(8,128)S(1)}, f32[2,32,128]{2,1,0:T(8,128)}, u32[]{:S(2)}) copy-start(f32[2,32,128]{2,1,0:T(8,128)} %constant.13.clone.twist_ref) | copy-start | bytes 98308
  23.0 44.1 %copy-start.2 = (bf16[4,256,256]{2,1,0:T(8,128)(2,1)S(1)}, bf16[4,256,256]{2,1,0:T(8,128)(2,1)}, u32[]{:S(2)}) copy-start(bf16[4,256,256]{2,1,0:T(8,128)(2,1)} %constant.14.clone.mats_hbm) | copy-start | bytes 1572868
  23.0 44.1 %copy-start.3 = (f32[2,2,2,64,128]{4,3,2,1,0:T(8,128)S(1)}, f32[2,2,2,64,128]{4,3,2,1,0:T(8,128)}, u32[]{:S(2)}) copy-start(f32[2,2,2,64,128]{4,3,2,1,0:T(8,128)} %constant.16.clone.behind_hbm) | copy-start | bytes 786436
  23.0 44.1 %copy-start.4 = (f32[2,2,128,128]{3,2,1,0:T(8,128)S(1)}, f32[2,2,128,128]{3,2,1,0:T(8,128)}, u32[]{:S(2)}) copy-start(f32[2,2,128,128]{3,2,1,0:T(8,128)} %constant.15.clone.ahead_hbm) | copy-start | bytes 786436
  23.1 44.1 %copy-start.6 = (f32[4]{0:T(128)S(1)}, f32[4]{0:T(128)}, u32[]{:S(2)}) copy-start(f32[4]{0:T(128)} %fresnel_ref.1) | copy-start | bytes 52
  23.1 44.1 %copy-start.7 = (f32[2]{0:T(128)S(1)}, f32[2]{0:T(128)}, u32[]{:S(2)}) copy-start(f32[2]{0:T(128)} %terms_ref.1) | copy-start | bytes 28
  67.2 26.3 %copy-start.1 = (bf16[4,2,256,256]{3,2,1,0:T(8,128)(2,1)S(1)}, bf16[4,2,256,256]{3,2,1,0:T(8,128)(2,1)}, u32[]{:S(2)}) copy-start(bf16[4,2,256,256]{3,2,1,0:T(8,128)(2,1)} %constant.17.clone.mats_ref) | copy-start | bytes 3145732

commit v3 on v2

--- a/solution.py
+++ b/solution.py
@@ -11,6 +11,7 @@
 
 N = 4096
 POS, NEG, ZERO, HALF = range(4)
+ORDER = [128 * (place % 2) + place // 2 for place in range(256)]
 F32 = jnp.float32
 BF16 = jnp.bfloat16
 
@@ -70,23 +71,25 @@
             [np.kron(eye8, sine), np.kron(eye8, cosine)],
         ]
     )
-    pick = np.kron(np.eye(4), np.ones((2, 1)))
-    twice = np.ones((1, 2))
+    pick = np.kron(np.ones((2, 2)), np.eye(4))
 
     def spread(block):
-        return np.kron(twice, np.kron(pick, block))
+        return np.kron(pick, block)
 
     inverse = np.block([[spread(cosine), spread(sine)], [spread(-sine), spread(cosine)]])
     lane = np.arange(128)
     within = lane % 16
     top = lane // 64
-    step = np.arange(128)[None, :, None] + 128 * np.arange(2)[:, None, None]
-    ahead = np.stack(turn(step * within, N)).astype(np.float32)
-    step = np.arange(64)[None, :, None] + 128 * np.arange(2)[:, None, None] + 64 * top
-    behind = np.stack(turn(step * within, N)).astype(np.float32)
-    step = np.arange(2)[:, None, None] + 2 * top
-    spin = np.stack(turn(step * np.arange(64)[None, :, None], 256)).astype(np.float32)
-    return np.concatenate([halves(forward), halves(inverse)]), ahead, np.stack([behind, spin])
+    parity = np.arange(2)[:, None, None]
+    ahead = np.stack(turn((2 * np.arange(128)[None, :, None] + parity) * within, N))
+    steps = np.arange(64)[None, :, None]
+    behind = [
+        turn((2 * steps + parity + 128 * h) * within + (32 * steps + 2048 * h) * top, N)
+        for h in range(2)
+    ]
+    spin = np.stack(turn(2 * np.arange(64)[:, None] + top, 256)).astype(np.float32)
+    ahead, behind = ahead.astype(np.float32), np.stack(behind).astype(np.float32)
+    return np.concatenate([halves(forward), halves(inverse)]), ahead, behind, spin
 
 
 def image_constants():
@@ -181,8 +184,8 @@
         for k1, line in enumerate(lines):
             if k1:
                 line = times(line, twist_ref[0, pl.ds(k1, 1), :], -twist_ref[1, pl.ds(k1, 1), :])
-            place = 32 * k1 if k1 < 16 else 512 + 32 * ((32 - k1) % 16 ^ 2)
-            rows = pl.ds(place + 16 * j, 16)
+            place = k1 if k1 < 16 else 16 + ((32 - k1) % 16 ^ 2)
+            rows = pl.ds(128 * (place // 4) + 64 * j + 16 * (place % 4), 16)
             for part in range(2):
                 high, low = split(line[part])
                 high_ref[rows, pl.ds(128 * part, 128)] = high
@@ -199,10 +202,11 @@
         for pair in range(2):
             at = slice(128 * pair, 128 * pair + 128)
             one, two = positive[:, at], negative[:, at]
-            even, odd = jnp.where(lane < 64, one, two), jnp.where(lane < 64, two, one)
+            low = (lane & 32) == 0
+            even, odd = jnp.where(low, one, two), jnp.where(low, two, one)
             if half == 0 and pair == 0:
-                even = jnp.where(lane < 32, mixed(ZERO, 0, 128), even)
-                even = jnp.where((lane & 96) == 64, mixed(HALF, 512, 128), even)
+                even = jnp.where((lane & 48) == 0, mixed(ZERO, 0, 128), even)
+                even = jnp.where((lane & 48) == 32, mixed(HALF, 512, 128), even)
             for side, block in enumerate([even, odd]):
                 quad = 4 * half + 2 * pair + side
                 out_ref[pl.ds(32 * quad, 32)] = block.reshape(32, 8, 128)
@@ -227,7 +231,8 @@
 
 
 def device_number():
-    return 8 * lax.axis_index("row") + lax.axis_index("col")
+    n = 8 * lax.axis_index("row") + lax.axis_index("col")
+    return 2 * (n % 128) + n // 128
 
 
 def arc_tangent(value):
@@ -247,18 +252,25 @@
     mats_hbm,
     ahead_hbm,
     behind_hbm,
+    spin_hbm,
     out_ref,
     work_ref,
     back_ref,
     mats_ref,
     ahead_ref,
     behind_ref,
+    spin_ref,
     sems,
 ):
     copies = [
         pltpu.make_async_copy(source, target, sems.at[k])
         for k, (source, target) in enumerate(
-            [(mats_hbm, mats_ref), (ahead_hbm, ahead_ref), (behind_hbm, behind_ref)]
+            [
+                (mats_hbm, mats_ref),
+                (ahead_hbm, ahead_ref),
+                (behind_hbm, behind_ref),
+                (spin_hbm, spin_ref),
+            ]
         )
     ]
     for copy in copies:
@@ -269,7 +281,6 @@
     lane = lax.broadcasted_iota(jnp.int32, (8, 128), 1)
     first = (sub & 2) == 0
     sign = jnp.where(first, 1.0, -1.0).astype(F32)
-    side = jnp.where(lane < 64, 1.0, -1.0).astype(F32)
 
     def shift(value, amount, axis):
         return pltpu.roll(value, amount, axis + value.ndim - 2)
@@ -282,15 +293,22 @@
         for na in range(16):
             n = 8 * na + nb
             one, two = field_ref[2 * n], field_ref[2 * n + 1]
-            lines.append(
-                (jnp.where(first, one, shift(two, 2, 0)), jnp.where(first, shift(one, 6, 0), two))
-            )
+            one, two = one + two, one - two
+            line = (jnp.where(first, one, shift(two, 2, 0)), jnp.where(first, shift(one, 6, 0), two))
+            if n:
+                angle = 2.0 * math.pi * n / 256
+                line = times(
+                    line,
+                    jnp.where(first, 1.0, math.cos(angle)).astype(F32),
+                    jnp.where(first, 0.0, -math.sin(angle)).astype(F32),
+                )
+            lines.append(line)
         for ka, line in enumerate(transform(lines, -1)):
             real, imag = turned(line, nb * ka, 128, -1)
             work_ref[0, ka, nb] = real
             work_ref[1, ka, nb] = imag
 
-    slot = (lane >> 5) ^ (2 * (quad & 1))
+    slot = ((lane >> 4) & 3) ^ (2 * (quad & 1))
     s = ((sub >> 2) << 1) | (sub & 1)
     positive = 4 * group + s
     base = 2 * group + (s & 1)
@@ -306,8 +324,8 @@
     v = jnp.where(v >= N // 2, v - N, v).astype(F32)
     v_square = v * v
     a2 = lane & 15
-    u_base = (64 * (sub & 2) + 256 * a2 - jnp.where(a2 >= 8, N, 0)).astype(F32)
-    later = (lane & 16) != 0
+    u_base = (((sub >> 1) & 1) + 256 * a2 - jnp.where(a2 >= 8, N, 0)).astype(F32)
+    later = lane >= 64
     rate_even = (0.5 / (N * N)) / jnp.where(later, fresnel_ref[2], fresnel_ref[0])
     rate_odd = (0.5 / (N * N)) / jnp.where(later, fresnel_ref[3], fresnel_ref[1])
     ratio = jnp.full((8, 128), terms_ref[0], F32)
@@ -336,17 +354,8 @@
         reals, imags = [], []
         for ka in range(4 * bunch, 4 * bunch + 4):
             lines = transform([(work_ref[0, ka, nb], work_ref[1, ka, nb]) for nb in range(8)], -1)
-            turned_lines = []
-            for kb, line in enumerate(lines):
-                angle = 2.0 * math.pi * (ka + 16 * kb) / 256
-                line = times(
-                    line,
-                    jnp.where(first, 1.0, math.cos(angle)).astype(F32),
-                    jnp.where(first, 0.0, -math.sin(angle)).astype(F32),
-                )
-                turned_lines.append(tuple(swap_pairs(z) + sign * z for z in line))
-            real = jnp.stack([z[0] for z in turned_lines])
-            imag = jnp.stack([z[1] for z in turned_lines])
+            real = jnp.stack([z[0] for z in lines])
+            imag = jnp.stack([z[1] for z in lines])
             cosine, sine = rows_of(ahead_ref, (), ka, 8, 16)
             real, imag = times((real, imag), cosine, -sine)
             reals.append(real.reshape(64, 128))
@@ -361,14 +370,13 @@
             rows = slice(64 * step, 64 * step + 64)
             real = mixed[rows, :128].reshape(8, 8, 128)
             imag = mixed[rows, 128:].reshape(8, 8, 128)
-            w1 = ka + 16 * lax.broadcasted_iota(jnp.int32, (8, 8, 128), 0)
+            w1 = 2 * ka + 32 * lax.broadcasted_iota(jnp.int32, (8, 8, 128), 0)
             u = u_base + w1.astype(F32)
             radius = u * u + v_square
             even = gain * sine_turns(radius * rate_even + offset)
             odd = gain * sine_turns(radius * rate_odd + offset)
             energy = even * even + odd * odd
-            other = jnp.where(later, shift(energy, 16, 1), shift(energy, 112, 1))
-            scale = 1.0 / (energy + other + floor)
+            scale = 1.0 / (energy + shift(energy, 64, 1) + floor)
             reals.append(((even * real + odd * imag) * scale).reshape(64, 128))
             imags.append(((even * imag - odd * real) * scale).reshape(64, 128))
         mixed = jnp.concatenate(
@@ -380,16 +388,9 @@
             rows = slice(64 * step, 64 * step + 64)
             real = mixed[rows, :128].reshape(8, 8, 128)
             imag = mixed[rows, 128:].reshape(8, 8, 128)
-            real = jnp.where(lane < 64, real[:4], real[4:])
-            imag = jnp.where(lane < 64, imag[:4], imag[4:])
-            cosine, sine = rows_of(behind_ref, (0,), ka, 4, 16)
-            real, imag = times((real, imag), cosine, sine)
-            real, imag = (swap_pairs(z) + sign * z for z in (real, imag))
-            corner = (lane >= 64) & jnp.logical_not(first)
-            real, imag = jnp.where(corner, -imag, real), jnp.where(corner, real, imag)
-            real, imag = (shift(z, 64, 1) + side * z for z in (real, imag))
-            cosine, sine = rows_of(behind_ref, (1,), ka, 4, 16)
-            real, imag = times((real, imag), cosine, sine)
+            early = times((real[:4], imag[:4]), *rows_of(behind_ref, (0,), ka, 4, 16))
+            later_half = times((real[4:], imag[4:]), *rows_of(behind_ref, (1,), ka, 4, 16))
+            real, imag = plus(early, later_half)
             back_ref[0, ka] = real
             back_ref[1, ka] = imag
 
@@ -414,7 +415,11 @@
 
     for na in range(8):
         lines = [(work_ref[0, na, wb], work_ref[1, na, wb]) for wb in range(8)]
-        for nb, (real, imag) in enumerate(transform(lines, 1)):
+        for nb, line in enumerate(transform(lines, 1)):
+            at = pl.ds(na + 8 * nb, 1)
+            cosine, sine = (jnp.broadcast_to(spin_ref[part, at], (8, 128)) for part in range(2))
+            line = times(line, jnp.where(first, 1.0, cosine), jnp.where(first, 0.0, sine))
+            real, imag = (swap_pairs(z) + sign * z for z in line)
             real, imag = real + partner(real), imag - partner(imag)
             packed = real + jnp.where(low_half, -shift(imag, 120, 1), shift(imag, 8, 1))
             crossed = shift(shift(packed, 64, 1), 4, 0)
@@ -484,8 +489,8 @@
 def filter_columns(field, fresnel, ctf_terms):
     constants = [jnp.asarray(c) for c in column_constants()]
     scratch = [pltpu.VMEM((2, 16, 8, 8, 128), F32), pltpu.VMEM((2, 16, 4, 8, 128), F32)]
-    scratch += [pltpu.VMEM(c.shape, c.dtype) for c in constants] + [pltpu.SemaphoreType.DMA((3,))]
-    spaces = [pltpu.SMEM] * 2 + [pltpu.VMEM] + [pltpu.HBM] * 3
+    scratch += [pltpu.VMEM(c.shape, c.dtype) for c in constants] + [pltpu.SemaphoreType.DMA((4,))]
+    spaces = [pltpu.SMEM] * 2 + [pltpu.VMEM] + [pltpu.HBM] * 4
     arguments = [fresnel, ctf_terms, field] + constants
     return call(columns_kernel, (64, 8, 128), scratch, arguments, spaces)
 
@@ -495,17 +500,23 @@
     return call(image_kernel, (8, 16, 512), [], arguments, [pltpu.VMEM] * 3)
 
 
-def exchange(field, axes):
-    return lax.all_to_all(field, axes, split_axis=0, concat_axis=0, tiled=True)
+def exchange(field):
+    return lax.all_to_all(field, "col", split_axis=0, concat_axis=0, tiled=True)
+
+
+def exchange_all(field):
+    return lax.all_to_all(
+        field, ("row", "col"), split_axis=0, concat_axis=0, tiled=True, axis_index_groups=[ORDER]
+    )
 
 
 def local(holograms, fresnel, ctf_terms):
     field = holograms.reshape(4, 8, 16, 512).transpose(1, 0, 2, 3)
-    field = image_rows(exchange(field, "col"))
-    field = filter_columns(exchange(field, ("row", "col")), fresnel, ctf_terms)
-    field = exchange(field.reshape(256, 2, 128), ("row", "col"))
+    field = image_rows(exchange(field))
+    field = filter_columns(exchange_all(field), fresnel, ctf_terms)
+    field = exchange_all(field.reshape(256, 2, 128))
     image = image_from(field.reshape(512, 128))
-    return exchange(image, "col").reshape(128, 512)
+    return exchange(image).reshape(128, 512)
 
 
 def solution(mesh):

time: 104 us -> 103 us (level)
  no operation moved by 1% of the time
where the time goes in v3:
time: 103 us
  blocking collectives  95 us (92%)
  Pallas kernels  5.7 us (6%)
  local copies, waits for them, and re-layouts  2.09 us (2%)
    all_to_all x2, blocking collectives, exchange_all(): lax.all_to_all(field, ('row', 'col'), split_axis=0, concat_axis=0, tiled=...  65.6 us
    all_to_all x2, blocking collectives, exchange(): return lax.all_to_all(field, 'col', split_axis=0, concat_axis=0, tiled=True)  29.4 us
    pallas_call x3, Pallas kernels, call(): pl.pallas_call(kernel, out_shape=jax.ShapeDtypeStruct(out_shape, F32), in...  5.7 us

profile of v3, /device:TPU:1, one launch (start us, length us, event | category | flops | bytes accessed | tf_op | source)
XLA Modules:
  0.0 103.0 jit_solution(652654899517165404)
XLA Ops:
  0.0 1.3 %copy.14 = f32[4,8,16,512]{3,2,0,1:T(8,128)S(1)} copy(f32[4,8,16,512]{3,2,1,0:T(8,128)} %bitcast.10) | data formatting | bytes 2097152 | tf_op jit(solution)/shard_map/reshape | solution.py:514
  1.3 0.0 copy-start
  1.3 0.0 copy-start.5
  1.4 20.4 %all_to_all.20.field_ref = f32[8,4,16,512]{3,2,1,0:T(8,128)S(1)} all-to-all(f32[8,4,16,512]{3,2,1,0:T(8,128)S(1)} %bitcast.9), channel_id=1, replica_groups=mesh['row'=32,'col'=8] {'col'}, dimensions={0} | all-to-all | bytes 2097152 | tf_op jit(solution)/shard_map/all_to_all | solution.py:504
  21.8 0.0 copy-done
  21.8 0.0 copy-done.5
  21.8 1.2 %shard_map.109 = f32[256,8,128]{2,1,0:T(8,128)S(1)} custom-call(f32[8,4,16,512]{3,2,1,0:T(8,128)S(1)} %all_to_all.20.field_ref, bf16[4,2,256,256]{3,2,1,0:T(8,128)(2,1)S(1)} %copy-done, f32[2,32,128]{2,1,0:T(8,128)S(1)} %copy-done.5), custom_call_target="tpu_custom_call" | custom-call | tf_op jit(solution)/shard_map/pallas_call | solution.py:473
  23.0 0.0 copy-start.2
  23.0 0.0 copy-start.3
  23.0 0.0 copy-start.4
  23.0 0.0 copy-start.6
  23.1 0.0 copy-start.7
  23.1 0.0 copy-start.8
  23.1 44.4 %all_to_all.21.field_ref = f32[256,8,128]{2,1,0:T(8,128)S(1)} all-to-all(f32[256,8,128]{2,1,0:T(8,128)S(1)} %shard_map.109), channel_id=1, replica_groups={{0,128,1,129,2,130,3,131,4,132,5,133,6,134,7,135,8,136,9,137,10,138,11,..., dimensions={0} | all-to-all | bytes 2097152 | tf_op jit(solution)/shard_map/all_to_all | solution.py:508
  67.5 0.0 copy-done.2
  67.5 0.0 copy-done.3
  67.5 0.0 copy-done.4
  67.5 0.0 copy-done.6
  67.5 0.0 copy-done.7
  67.5 0.0 copy-done.8
  67.5 0.0 copy-start.1
  67.5 3.9 %shard_map.110 = f32[64,8,128]{2,1,0:T(8,128)S(1)} custom-call(f32[4]{0:T(128)S(1)} %copy-done.7, f32[2]{0:T(128)S(1)} %copy-done.8, f32[256,8,128]{2,1,0:T(8,128)S(1)} %all_to_all.21.field_ref, bf16[4,256,256]{2,1,0:T(8,128)(2,1)S(1)} %copy-done.2, f32[2,2,128,128]{3,2,1,0:T(8,128)S(1)} %copy-done.4, f32[2,2,2,64,128]{4,3,2,1,0:T(8,128)S(1)} %copy-done.3, ...), custom_call_target="tpu_custom_call" | custom-call | tf_op jit(solution)/shard_map/pallas_call | solution.py:473
  71.4 21.3 %all_to_all.22 = f32[256,2,128]{2,1,0:T(2,128)S(1)} all-to-all(f32[256,2,128]{2,1,0:T(2,128)S(1)} %bitcast.7), channel_id=1, replica_groups={{0,128,1,129,2,130,3,131,4,132,5,133,6,134,7,135,8,136,9,137,10,138,11,..., dimensions={0} | all-to-all | bytes 524288 | tf_op jit(solution)/shard_map/all_to_all | solution.py:508
  92.7 0.0 copy-done.1
  92.7 0.6 shard_map.111
  93.3 9.0 %all_to_all.23 = f32[8,16,512]{2,1,0:T(8,128)S(1)} all-to-all(f32[8,16,512]{2,1,0:T(8,128)S(1)} %shard_map.111), channel_id=1, replica_groups=mesh['row'=32,'col'=8] {'col'}, dimensions={0} | all-to-all | bytes 524288 | tf_op jit(solution)/shard_map/all_to_all | solution.py:504
  102.2 0.7 copy.16
Async XLA Ops:
  1.3 20.5 %copy-start = (bf16[4,2,256,256]{3,2,1,0:T(8,128)(2,1)S(1)}, bf16[4,2,256,256]{3,2,1,0:T(8,128)(2,1)}, u32[]{:S(2)}) copy-start(bf16[4,2,256,256]{3,2,1,0:T(8,128)(2,1)} %constant.14.clone.mats_ref) | copy-start | bytes 3145732
  1.3 20.4 %copy-start.5 = (f32[2,32,128]{2,1,0:T(8,128)S(1)}, f32[2,32,128]{2,1,0:T(8,128)}, u32[]{:S(2)}) copy-start(f32[2,32,128]{2,1,0:T(8,128)} %constant.15.clone.twist_ref) | copy-start | bytes 98308
  23.0 44.5 %copy-start.2 = (bf16[4,256,256]{2,1,0:T(8,128)(2,1)S(1)}, bf16[4,256,256]{2,1,0:T(8,128)(2,1)}, u32[]{:S(2)}) copy-start(bf16[4,256,256]{2,1,0:T(8,128)(2,1)} %constant.16.clone.mats_hbm) | copy-start | bytes 1572868
  23.0 44.5 %copy-start.3 = (f32[2,2,2,64,128]{4,3,2,1,0:T(8,128)S(1)}, f32[2,2,2,64,128]{4,3,2,1,0:T(8,128)}, u32[]{:S(2)}) copy-start(f32[2,2,2,64,128]{4,3,2,1,0:T(8,128)} %constant.18.clone.behind_hbm) | copy-start | bytes 786436
  23.0 44.4 %copy-start.4 = (f32[2,2,128,128]{3,2,1,0:T(8,128)S(1)}, f32[2,2,128,128]{3,2,1,0:T(8,128)}, u32[]{:S(2)}) copy-start(f32[2,2,128,128]{3,2,1,0:T(8,128)} %constant.17.clone.ahead_hbm) | copy-start | bytes 786436
  23.0 44.4 %copy-start.6 = (f32[2,64,128]{2,1,0:T(8,128)S(1)}, f32[2,64,128]{2,1,0:T(8,128)}, u32[]{:S(2)}) copy-start(f32[2,64,128]{2,1,0:T(8,128)} %constant.19.clone.spin_hbm) | copy-start | bytes 196612
  23.1 44.4 %copy-start.7 = (f32[4]{0:T(128)S(1)}, f32[4]{0:T(128)}, u32[]{:S(2)}) copy-start(f32[4]{0:T(128)} %fresnel_ref.1) | copy-start | bytes 52
  23.1 44.4 %copy-start.8 = (f32[2]{0:T(128)S(1)}, f32[2]{0:T(128)}, u32[]{:S(2)}) copy-start(f32[2]{0:T(128)} %terms_ref.1) | copy-start | bytes 28
  67.5 25.2 %copy-start.1 = (bf16[4,2,256,256]{3,2,1,0:T(8,128)(2,1)S(1)}, bf16[4,2,256,256]{3,2,1,0:T(8,128)(2,1)}, u32[]{:S(2)}) copy-start(bf16[4,2,256,256]{3,2,1,0:T(8,128)(2,1)} %constant.20.clone.mats_ref) | copy-start | bytes 3145732

commit v4 on v3

--- a/solution.py
+++ b/solution.py
@@ -88,6 +88,7 @@
         for h in range(2)
     ]
     spin = np.stack(turn(2 * np.arange(64)[:, None] + top, 256)).astype(np.float32)
+    ahead = np.repeat(ahead[:, [0, 1, 0, 1]].transpose(0, 2, 1, 3), 2, 2)
     ahead, behind = ahead.astype(np.float32), np.stack(behind).astype(np.float32)
     return np.concatenate([halves(forward), halves(inverse)]), ahead, behind, spin
 
@@ -249,32 +250,14 @@
     fresnel_ref,
     terms_ref,
     field_ref,
-    mats_hbm,
-    ahead_hbm,
-    behind_hbm,
-    spin_hbm,
-    out_ref,
-    work_ref,
-    back_ref,
     mats_ref,
     ahead_ref,
     behind_ref,
     spin_ref,
-    sems,
+    out_ref,
+    work_ref,
+    back_ref,
 ):
-    copies = [
-        pltpu.make_async_copy(source, target, sems.at[k])
-        for k, (source, target) in enumerate(
-            [
-                (mats_hbm, mats_ref),
-                (ahead_hbm, ahead_ref),
-                (behind_hbm, behind_ref),
-                (spin_hbm, spin_ref),
-            ]
-        )
-    ]
-    for copy in copies:
-        copy.start()
     device = device_number()
     quad, group = device // 32, device % 32
     sub = lax.broadcasted_iota(jnp.int32, (8, 128), 0)
@@ -331,7 +314,7 @@
     ratio = jnp.full((8, 128), terms_ref[0], F32)
     offset = arc_tangent(ratio) * (0.5 / math.pi)
     gain = 2.0 * jnp.sqrt(1.0 + ratio * ratio)
-    floor = terms_ref[1]
+    floor = terms_ref[1] / gain
 
     def rows_of(table, which, start, count, stride):
         picked = []
@@ -345,8 +328,6 @@
             picked.append(jnp.stack(tiles))
         return picked
 
-    for copy in copies:
-        copy.wait()
     forward = (mats_ref[0], mats_ref[1])
     inverse = (mats_ref[2], mats_ref[3])
     natural = ((1,), (0,))
@@ -356,7 +337,9 @@
             lines = transform([(work_ref[0, ka, nb], work_ref[1, ka, nb]) for nb in range(8)], -1)
             real = jnp.stack([z[0] for z in lines])
             imag = jnp.stack([z[1] for z in lines])
-            cosine, sine = rows_of(ahead_ref, (), ka, 8, 16)
+            cosine, sine = (
+                jnp.stack([ahead_ref[part, ka + 16 * kb] for kb in range(8)]) for part in range(2)
+            )
             real, imag = times((real, imag), cosine, -sine)
             reals.append(real.reshape(64, 128))
             imags.append(imag.reshape(64, 128))
@@ -370,15 +353,15 @@
             rows = slice(64 * step, 64 * step + 64)
             real = mixed[rows, :128].reshape(8, 8, 128)
             imag = mixed[rows, 128:].reshape(8, 8, 128)
-            w1 = 2 * ka + 32 * lax.broadcasted_iota(jnp.int32, (8, 8, 128), 0)
-            u = u_base + w1.astype(F32)
-            radius = u * u + v_square
-            even = gain * sine_turns(radius * rate_even + offset)
-            odd = gain * sine_turns(radius * rate_odd + offset)
-            energy = even * even + odd * odd
-            scale = 1.0 / (energy + shift(energy, 64, 1) + floor)
-            reals.append(((even * real + odd * imag) * scale).reshape(64, 128))
-            imags.append(((even * imag - odd * real) * scale).reshape(64, 128))
+            for kb in range(8):
+                u = u_base + float(2 * ka + 32 * kb)
+                radius = u * u + v_square
+                even = sine_turns(radius * rate_even + offset)
+                odd = sine_turns(radius * rate_odd + offset)
+                energy = even * even + odd * odd
+                scale = 1.0 / (gain * (energy + shift(energy, 64, 1)) + floor)
+                reals.append((even * real[kb] + odd * imag[kb]) * scale)
+                imags.append((even * imag[kb] - odd * real[kb]) * scale)
         mixed = jnp.concatenate(
             [jnp.concatenate(reals, 0), jnp.concatenate(imags, 0)], 1
         )
@@ -489,8 +472,7 @@
 def filter_columns(field, fresnel, ctf_terms):
     constants = [jnp.asarray(c) for c in column_constants()]
     scratch = [pltpu.VMEM((2, 16, 8, 8, 128), F32), pltpu.VMEM((2, 16, 4, 8, 128), F32)]
-    scratch += [pltpu.VMEM(c.shape, c.dtype) for c in constants] + [pltpu.SemaphoreType.DMA((4,))]
-    spaces = [pltpu.SMEM] * 2 + [pltpu.VMEM] + [pltpu.HBM] * 4
+    spaces = [pltpu.SMEM] * 2 + [pltpu.VMEM] * 5
     arguments = [fresnel, ctf_terms, field] + constants
     return call(columns_kernel, (64, 8, 128), scratch, arguments, spaces)
 

time: 103 us -> 103 us (level)
  no operation moved by 1% of the time
where the time goes in v4:
time: 103 us
  blocking collectives  95 us (92%)
  Pallas kernels  5.55 us (5%)
  local copies, waits for them, and re-layouts  2.09 us (2%)
    all_to_all x2, blocking collectives, exchange_all(): lax.all_to_all(field, ('row', 'col'), split_axis=0, concat_axis=0, tiled=...  65.6 us
    all_to_all x2, blocking collectives, exchange(): return lax.all_to_all(field, 'col', split_axis=0, concat_axis=0, tiled=True)  29.4 us
    pallas_call x3, Pallas kernels, call(): pl.pallas_call(kernel, out_shape=jax.ShapeDtypeStruct(out_shape, F32), in...  5.55 us

profile of v4, /device:TPU:1, one launch (start us, length us, event | category | flops | bytes accessed | tf_op | source)
XLA Modules:
  0.0 102.8 jit_solution(26563137739910081)
XLA Ops:
  0.0 1.3 %copy.14 = f32[4,8,16,512]{3,2,0,1:T(8,128)S(1)} copy(f32[4,8,16,512]{3,2,1,0:T(8,128)} %bitcast.10) | data formatting | bytes 2097152 | tf_op jit(solution)/shard_map/reshape | solution.py:496
  1.3 0.0 copy-start
  1.3 0.0 copy-start.5
  1.4 20.4 %all_to_all.20.field_ref = f32[8,4,16,512]{3,2,1,0:T(8,128)S(1)} all-to-all(f32[8,4,16,512]{3,2,1,0:T(8,128)S(1)} %bitcast.9), channel_id=1, replica_groups=mesh['row'=32,'col'=8] {'col'}, dimensions={0} | all-to-all | bytes 2097152 | tf_op jit(solution)/shard_map/all_to_all | solution.py:486
  21.8 0.0 copy-done
  21.8 0.0 copy-done.5
  21.8 1.2 %shard_map.109 = f32[256,8,128]{2,1,0:T(8,128)S(1)} custom-call(f32[8,4,16,512]{3,2,1,0:T(8,128)S(1)} %all_to_all.20.field_ref, bf16[4,2,256,256]{3,2,1,0:T(8,128)(2,1)S(1)} %copy-done, f32[2,32,128]{2,1,0:T(8,128)S(1)} %copy-done.5), custom_call_target="tpu_custom_call" | custom-call | tf_op jit(solution)/shard_map/pallas_call | solution.py:456
  23.0 0.0 copy-start.2
  23.0 0.0 copy-start.3
  23.0 0.0 copy-start.4
  23.0 0.0 copy-start.6
  23.1 0.0 copy-start.7
  23.1 0.0 copy-start.8
  23.1 44.4 %all_to_all.21.field_ref = f32[256,8,128]{2,1,0:T(8,128)S(1)} all-to-all(f32[256,8,128]{2,1,0:T(8,128)S(1)} %shard_map.109), channel_id=1, replica_groups={{0,128,1,129,2,130,3,131,4,132,5,133,6,134,7,135,8,136,9,137,10,138,11,..., dimensions={0} | all-to-all | bytes 2097152 | tf_op jit(solution)/shard_map/all_to_all | solution.py:490
  67.5 0.0 copy-done.2
  67.5 0.0 copy-done.3
  67.5 0.0 copy-done.4
  67.5 0.0 copy-done.6
  67.5 0.0 copy-done.7
  67.5 0.0 copy-done.8
  67.5 0.0 copy-start.1
  67.5 3.7 %shard_map.110 = f32[64,8,128]{2,1,0:T(8,128)S(1)} custom-call(f32[4]{0:T(128)S(1)} %copy-done.7, f32[2]{0:T(128)S(1)} %copy-done.8, f32[256,8,128]{2,1,0:T(8,128)S(1)} %all_to_all.21.field_ref, bf16[4,256,256]{2,1,0:T(8,128)(2,1)S(1)} %copy-done.3, f32[2,128,8,128]{3,2,1,0:T(8,128)S(1)} %copy-done.2, f32[2,2,2,64,128]{4,3,2,1,0:T(8,128)S(1)} %copy-done.4, ...), custom_call_target="tpu_custom_call" | custom-call | tf_op jit(solution)/shard_map/pallas_call | solution.py:456
  71.3 21.3 %all_to_all.22 = f32[256,2,128]{2,1,0:T(2,128)S(1)} all-to-all(f32[256,2,128]{2,1,0:T(2,128)S(1)} %bitcast.7), channel_id=1, replica_groups={{0,128,1,129,2,130,3,131,4,132,5,133,6,134,7,135,8,136,9,137,10,138,11,..., dimensions={0} | all-to-all | bytes 524288 | tf_op jit(solution)/shard_map/all_to_all | solution.py:490
  92.5 0.0 copy-done.1
  92.5 0.6 shard_map.111
  93.1 9.0 %all_to_all.23 = f32[8,16,512]{2,1,0:T(8,128)S(1)} all-to-all(f32[8,16,512]{2,1,0:T(8,128)S(1)} %shard_map.111), channel_id=1, replica_groups=mesh['row'=32,'col'=8] {'col'}, dimensions={0} | all-to-all | bytes 524288 | tf_op jit(solution)/shard_map/all_to_all | solution.py:486
  102.1 0.7 copy.16
Async XLA Ops:
  1.3 20.5 %copy-start = (bf16[4,2,256,256]{3,2,1,0:T(8,128)(2,1)S(1)}, bf16[4,2,256,256]{3,2,1,0:T(8,128)(2,1)}, u32[]{:S(2)}) copy-start(bf16[4,2,256,256]{3,2,1,0:T(8,128)(2,1)} %constant.14.clone.mats_ref) | copy-start | bytes 3145732
  1.3 20.4 %copy-start.5 = (f32[2,32,128]{2,1,0:T(8,128)S(1)}, f32[2,32,128]{2,1,0:T(8,128)}, u32[]{:S(2)}) copy-start(f32[2,32,128]{2,1,0:T(8,128)} %constant.15.clone.twist_ref) | copy-start | bytes 98308
  23.0 44.5 %copy-start.2 = (f32[2,128,8,128]{3,2,1,0:T(8,128)S(1)}, f32[2,128,8,128]{3,2,1,0:T(8,128)}, u32[]{:S(2)}) copy-start(f32[2,128,8,128]{3,2,1,0:T(8,128)} %constant.17.clone.ahead_ref) | copy-start | bytes 3145732
  23.0 44.5 %copy-start.3 = (bf16[4,256,256]{2,1,0:T(8,128)(2,1)S(1)}, bf16[4,256,256]{2,1,0:T(8,128)(2,1)}, u32[]{:S(2)}) copy-start(bf16[4,256,256]{2,1,0:T(8,128)(2,1)} %constant.16.clone.mats_ref) | copy-start | bytes 1572868
  23.0 44.4 %copy-start.4 = (f32[2,2,2,64,128]{4,3,2,1,0:T(8,128)S(1)}, f32[2,2,2,64,128]{4,3,2,1,0:T(8,128)}, u32[]{:S(2)}) copy-start(f32[2,2,2,64,128]{4,3,2,1,0:T(8,128)} %constant.18.clone.behind_ref) | copy-start | bytes 786436
  23.0 44.4 %copy-start.6 = (f32[2,64,128]{2,1,0:T(8,128)S(1)}, f32[2,64,128]{2,1,0:T(8,128)}, u32[]{:S(2)}) copy-start(f32[2,64,128]{2,1,0:T(8,128)} %constant.19.clone.spin_ref) | copy-start | bytes 196612
  23.1 44.4 %copy-start.7 = (f32[4]{0:T(128)S(1)}, f32[4]{0:T(128)}, u32[]{:S(2)}) copy-start(f32[4]{0:T(128)} %fresnel_ref.1) | copy-start | bytes 52
  23.1 44.4 %copy-start.8 = (f32[2]{0:T(128)S(1)}, f32[2]{0:T(128)}, u32[]{:S(2)}) copy-start(f32[2]{0:T(128)} %terms_ref.1) | copy-start | bytes 28
  67.5 25.0 %copy-start.1 = (bf16[4,2,256,256]{3,2,1,0:T(8,128)(2,1)S(1)}, bf16[4,2,256,256]{3,2,1,0:T(8,128)(2,1)}, u32[]{:S(2)}) copy-start(bf16[4,2,256,256]{3,2,1,0:T(8,128)(2,1)} %constant.20.clone.mats_ref) | copy-start | bytes 3145732

commit v5 on v4

--- a/solution.py
+++ b/solution.py
@@ -482,6 +482,26 @@
     return call(image_kernel, (8, 16, 512), [], arguments, [pltpu.VMEM] * 3)
 
 
+STEPS = [(2, 1), (0, 1), (2, 0), (1, 1), (3, 0), (3, 1), (1, 0)]
+
+
+def ring_exchange(field):
+    me = lax.axis_index("col")
+    own = lax.dynamic_slice_in_dim(field, me, 1, 1)
+    result = jnp.zeros((8, 4, 16, 512), F32)
+    result = lax.dynamic_update_slice_in_dim(result, own.transpose(1, 0, 2, 3), me, 0)
+    for step, flip in STEPS:
+
+        def there(place, sign):
+            return (place // 4 ^ flip) * 4 + (place + sign * step) % 4
+
+        chunk = lax.dynamic_slice_in_dim(field, there(me, 1), 1, 1)
+        pairs = [(place, there(place, 1)) for place in range(8)]
+        chunk = lax.ppermute(chunk.reshape(1, 4, 16, 512), "col", pairs)
+        result = lax.dynamic_update_slice_in_dim(result, chunk, there(me, -1), 0)
+    return result
+
+
 def exchange(field):
     return lax.all_to_all(field, "col", split_axis=0, concat_axis=0, tiled=True)
 
@@ -493,8 +513,7 @@
 
 
 def local(holograms, fresnel, ctf_terms):
-    field = holograms.reshape(4, 8, 16, 512).transpose(1, 0, 2, 3)
-    field = image_rows(exchange(field))
+    field = image_rows(ring_exchange(holograms.reshape(4, 8, 16, 512)))
     field = filter_columns(exchange_all(field), fresnel, ctf_terms)
     field = exchange_all(field.reshape(256, 2, 128))
     image = image_from(field.reshape(512, 128))

time: 103 us -> 102 us (level)
  blocking collectives: 95 us -> 75.8 us
  starting transfers between devices: 0 us -> 10.6 us
  waiting for transfers between devices: 0 us -> 4.91 us
  local copies, waits for them, and re-layouts: 2.09 us -> 4.19 us
    all_to_all x2 -> x1, blocking collectives: 29.4 us -> 8.95 us  [exchange(): return lax.all_to_all(field, 'col', split_axis=0, concat_axis=0, tiled=True)]
    ppermute x0 -> x7, starting transfers between devices: none -> 10.6 us  [ring_exchange(): chunk = lax.ppermute(chunk.reshape(1, 4, 16, 512), 'col', pairs)]
    ppermute x0 -> x7, waiting for transfers between devices: none -> 4.91 us  [ring_exchange(): chunk = lax.ppermute(chunk.reshape(1, 4, 16, 512), 'col', pairs)]
    dynamic_update_slice x0 -> x8, local copies, waits for them, and re-layouts: none -> 2 us  [the longest x1 1.01 us: ring_exchange(): lax.dynamic_update_slice_in_dim(result, own.transpose(1, 0, 2, 3), me, 0)]
    all_to_all x2, blocking collectives: 65.6 us -> 66.9 us  [exchange_all(): lax.all_to_all(field, ('row', 'col'), split_axis=0, concat_axis=0, tiled=...]
  transfers between devices with their start and end apart: 0 -> 7, of which waited for: 0 -> 3; matrix products, arithmetic and copies ran while one was open for 0% -> 2% of each run, Pallas kernels for 0% -> 0%
where the time goes in v5:
time: 102 us; the launch traced here: 101 us
  blocking collectives  75.8 us (74%)
  starting transfers between devices  10.6 us (10%)
  Pallas kernels  5.5 us (5%)
  waiting for transfers between devices  4.91 us (5%)
  local copies, waits for them, and re-layouts  4.19 us (4%)
    all_to_all x2, blocking collectives, exchange_all(): lax.all_to_all(field, ('row', 'col'), split_axis=0, concat_axis=0, tiled=...  66.9 us
    ppermute x7, starting transfers between devices, ring_exchange(): chunk = lax.ppermute(chunk.reshape(1, 4, 16, 512), 'col', pairs)  10.6 us
    all_to_all x1, blocking collectives, exchange(): return lax.all_to_all(field, 'col', split_axis=0, concat_axis=0, tiled=True)  8.95 us
    pallas_call x3, Pallas kernels, call(): pl.pallas_call(kernel, out_shape=jax.ShapeDtypeStruct(out_shape, F32), in...  5.5 us
    ppermute x7, waiting for transfers between devices, ring_exchange(): chunk = lax.ppermute(chunk.reshape(1, 4, 16, 512), 'col', pairs)  4.91 us
  transfers between devices with their start and end apart: 7, of which 3 were waited for; matrix products, arithmetic and copies ran while one was open for 2% of the time, Pallas kernels for 0%

profile of v5, /device:TPU:1, one launch (start us, length us, event | category | flops | bytes accessed | tf_op | source)
XLA Modules:
  0.0 101.3 jit_solution(163059704698041272)
XLA Ops:
  0.0 1.3 %dynamic-slice_bitcast_fusion = (f32[1,4,16,512]{3,2,1,0:T(8,128)S(1)}, f32[1,4,16,512]{3,2,1,0:T(8,128)S(1)}, f32[1,4,16,512]{3,2,1,0:T(8,128)S(1)}, f32[1,4,16...) fusion(f32[4,8,16,512]{3,2,1,0:T(8,128)} %bitcast.38, ...), kind=kLoop, calls=%fused_computation.1 | loop fusion | bytes 1835036 | tf_op jit(solution)/shard_map/reshape | solution.py:500
  1.3 5.0 %collective-permute-start = (f32[1,4,16,512]{3,2,1,0:T(8,128)S(1)}, f32[1,4,16,512]{3,2,1,0:T(8,128)}, u32[]{:S(2)}, u32[]{:S(2)}) collective-permute-start(f32[1,4,16,512]{3,2,1,0:T(8,128)S(1)} %get-tuple-element.11), channel_id=1, source_target_pairs={{0,6},{1,7},{2,4},{3,5},{4,2},{5,3},{6,0},{7,1},{8,14},{9,15},{10,... | collective-permute-start | bytes 393224 | tf_op jit(solution)/shard_map/ppermute | solution.py:500
  6.3 0.0 collective-permute-start.1
  6.3 0.4 collective-permute-start.2
  6.7 2.2 %collective-permute-start.3 = (f32[1,4,16,512]{3,2,1,0:T(8,128)S(1)}, f32[1,4,16,512]{3,2,1,0:T(8,128)S(1)}, u32[]{:S(2)}, u32[]{:S(2)}) collective-permute-start(f32[1,4,16,512]{3,2,1,0:T(8,128)S(1)} %get-tuple-element.8), channel_id=1, source_target_pairs={{0,5},{1,6},{2,7},{3,4},{4,1},{5,2},{6,3},{7,0},{8,13},{9,14},{10,... | collective-permute-start | bytes 393224 | tf_op jit(solution)/shard_map/ppermute | solution.py:500
  9.0 1.5 %collective-permute-start.4 = (f32[1,4,16,512]{3,2,1,0:T(8,128)S(1)}, f32[1,4,16,512]{3,2,1,0:T(8,128)S(1)}, u32[]{:S(2)}, u32[]{:S(2)}) collective-permute-start(f32[1,4,16,512]{3,2,1,0:T(8,128)S(1)} %get-tuple-element.7), channel_id=1, source_target_pairs={{0,3},{1,0},{2,1},{3,2},{4,7},{5,4},{6,5},{7,6},{8,11},{9,8},{10,9... | collective-permute-start | bytes 393224 | tf_op jit(solution)/shard_map/ppermute | solution.py:500
  10.4 0.1 broadcast_in_dim.3
  10.5 0.0 copy-start
  10.6 1.0 bitcast_dynamic-update-slice_fusion
  11.7 0.0 collective-permute-done
  11.7 1.3 %collective-permute-start.5 = (f32[1,4,16,512]{3,2,1,0:T(8,128)S(1)}, f32[1,4,16,512]{3,2,1,0:T(8,128)S(1)}, u32[]{:S(2)}, u32[]{:S(2)}) collective-permute-start(f32[1,4,16,512]{3,2,1,0:T(8,128)S(1)} %get-tuple-element.6), channel_id=1, source_target_pairs={{0,7},{1,4},{2,5},{3,6},{4,3},{5,0},{6,1},{7,2},{8,15},{9,12},{10,... | collective-permute-start | bytes 393224 | tf_op jit(solution)/shard_map/ppermute | solution.py:500
  12.9 0.9 constant_dynamic-update-slice_fusion.5
  13.9 0.0 collective-permute-done.1
  13.9 0.2 collective-permute-start.6
  14.1 3.1 %collective-permute-done.2 = f32[1,4,16,512]{3,2,1,0:T(8,128)S(1)} collective-permute-done((f32[1,4,16,512]{3,2,1,0:T(8,128)S(1)}, f32[1,4,16,512]{3,2,1,0:T(8,128)S(1)}, u32[]{:S(2)}, u32[]{:S(2)}) %collective-permute-start.2) | collective-permute-done | bytes 131104 | tf_op jit(solution)/shard_map/ppermute | solution.py:500
  17.2 0.0 collective-permute-done.3
  17.3 0.0 collective-permute-done.4
  17.3 0.3 collective-permute-done.5
  17.6 0.0 copy-start.5
  17.6 1.5 %collective-permute-done.6 = f32[1,4,16,512]{3,2,1,0:T(8,128)S(1)} collective-permute-done((f32[1,4,16,512]{3,2,1,0:T(8,128)S(1)}, f32[1,4,16,512]{3,2,1,0:T(8,128)S(1)}, u32[]{:S(2)}, u32[]{:S(2)}) %collective-permute-start.6) | collective-permute-done | bytes 131104 | tf_op jit(solution)/shard_map/ppermute | solution.py:500
  19.1 0.0 copy-done
  19.1 0.0 copy-done.5
  19.1 1.2 %shard_map.109 = f32[256,8,128]{2,1,0:T(8,128)S(1)} custom-call(f32[8,4,16,512]{3,2,1,0:T(8,128)S(1)} %constant_dynamic-update-slice_fusion.6.field_ref, bf16[4,2,256,256]{3,2,1,0:T(8,128)(2,1)S(1)} %copy-done, f32[2,32,128]{2,1,0:T(8,128)S(1)} %copy-done.5), custom_call_target="tpu_custom_call" | custom-call | tf_op jit(solution)/shard_map/pallas_call | solution.py:456
  20.4 0.0 copy-start.2
  20.4 0.0 copy-start.3
  20.4 0.0 copy-start.4
  20.4 0.0 copy-start.6
  20.4 0.0 copy-start.7
  20.4 0.0 copy-start.8
  20.4 45.6 %all_to_all.15.field_ref = f32[256,8,128]{2,1,0:T(8,128)S(1)} all-to-all(f32[256,8,128]{2,1,0:T(8,128)S(1)} %shard_map.109), channel_id=1, replica_groups={{0,128,1,129,2,130,3,131,4,132,5,133,6,134,7,135,8,136,9,137,10,138,11,..., dimensions={0} | all-to-all | bytes 2097152 | tf_op jit(solution)/shard_map/all_to_all | solution.py:510
  66.1 0.0 copy-done.2
  66.1 0.0 copy-done.3
  66.1 0.0 copy-done.4
  66.1 0.0 copy-done.6
  66.1 0.0 copy-done.7
  66.1 0.0 copy-done.8
  66.1 0.0 copy-start.1
  66.1 3.7 %shard_map.110 = f32[64,8,128]{2,1,0:T(8,128)S(1)} custom-call(f32[4]{0:T(128)S(1)} %copy-done.7, f32[2]{0:T(128)S(1)} %copy-done.8, f32[256,8,128]{2,1,0:T(8,128)S(1)} %all_to_all.15.field_ref, bf16[4,256,256]{2,1,0:T(8,128)(2,1)S(1)} %copy-done.3, f32[2,128,8,128]{3,2,1,0:T(8,128)S(1)} %copy-done.2, f32[2,2,2,64,128]{4,3,2,1,0:T(8,128)S(1)} %copy-done.4, ...), custom_call_target="tpu_custom_call" | custom-call | tf_op jit(solution)/shard_map/pallas_call | solution.py:456
  69.8 21.3 %all_to_all.16 = f32[256,2,128]{2,1,0:T(2,128)S(1)} all-to-all(f32[256,2,128]{2,1,0:T(2,128)S(1)} %bitcast.36), channel_id=1, replica_groups={{0,128,1,129,2,130,3,131,4,132,5,133,6,134,7,135,8,136,9,137,10,138,11,..., dimensions={0} | all-to-all | bytes 524288 | tf_op jit(solution)/shard_map/all_to_all | solution.py:510
  91.1 0.0 copy-done.1
  91.1 0.6 shard_map.111
  91.7 9.0 %all_to_all.17 = f32[8,16,512]{2,1,0:T(8,128)S(1)} all-to-all(f32[8,16,512]{2,1,0:T(8,128)S(1)} %shard_map.111), channel_id=1, replica_groups=mesh['row'=32,'col'=8] {'col'}, dimensions={0} | all-to-all | bytes 524288 | tf_op jit(solution)/shard_map/all_to_all | solution.py:506
  100.6 0.7 copy.37
  (6 shorter events, 0.1 us)
Async XLA Ops:
  1.3 10.3 %collective-permute-start = (f32[1,4,16,512]{3,2,1,0:T(8,128)S(1)}, f32[1,4,16,512]{3,2,1,0:T(8,128)}, u32[]{:S(2)}, u32[]{:S(2)}) collective-permute-start(f32[1,4,16,512]{3,2,1,0:T(8,128)S(1)} %get-tuple-element.11), channel_id=1, source_target_pairs={{0,6},{1,7},{2,4},{3,5},{4,2},{5,3},{6,0},{7,1},{8,14},{9,15},{10,... | collective-permute-start | bytes 393224 | tf_op jit(solution)/shard_map/ppermute | solution.py:500
  6.3 7.5 %collective-permute-start.1 = (f32[1,4,16,512]{3,2,1,0:T(8,128)S(1)}, f32[1,4,16,512]{3,2,1,0:T(8,128)S(1)}, u32[]{:S(2)}, u32[]{:S(2)}) collective-permute-start(f32[1,4,16,512]{3,2,1,0:T(8,128)S(1)} %get-tuple-element.10), channel_id=1, source_target_pairs={{0,4},{1,5},{2,6},{3,7},{4,0},{5,1},{6,2},{7,3},{8,12},{9,13},{10,... | collective-permute-start | bytes 393224 | tf_op jit(solution)/shard_map/ppermute | solution.py:500
  6.3 10.9 %collective-permute-start.2 = (f32[1,4,16,512]{3,2,1,0:T(8,128)S(1)}, f32[1,4,16,512]{3,2,1,0:T(8,128)S(1)}, u32[]{:S(2)}, u32[]{:S(2)}) collective-permute-start(f32[1,4,16,512]{3,2,1,0:T(8,128)S(1)} %get-tuple-element.9), channel_id=1, source_target_pairs={{0,2},{1,3},{2,0},{3,1},{4,6},{5,7},{6,4},{7,5},{8,10},{9,11},{10,... | collective-permute-start | bytes 393224 | tf_op jit(solution)/shard_map/ppermute | solution.py:500
  6.7 10.5 %collective-permute-start.3 = (f32[1,4,16,512]{3,2,1,0:T(8,128)S(1)}, f32[1,4,16,512]{3,2,1,0:T(8,128)S(1)}, u32[]{:S(2)}, u32[]{:S(2)}) collective-permute-start(f32[1,4,16,512]{3,2,1,0:T(8,128)S(1)} %get-tuple-element.8), channel_id=1, source_target_pairs={{0,5},{1,6},{2,7},{3,4},{4,1},{5,2},{6,3},{7,0},{8,13},{9,14},{10,... | collective-permute-start | bytes 393224 | tf_op jit(solution)/shard_map/ppermute | solution.py:500
  9.0 8.3 %collective-permute-start.4 = (f32[1,4,16,512]{3,2,1,0:T(8,128)S(1)}, f32[1,4,16,512]{3,2,1,0:T(8,128)S(1)}, u32[]{:S(2)}, u32[]{:S(2)}) collective-permute-start(f32[1,4,16,512]{3,2,1,0:T(8,128)S(1)} %get-tuple-element.7), channel_id=1, source_target_pairs={{0,3},{1,0},{2,1},{3,2},{4,7},{5,4},{6,5},{7,6},{8,11},{9,8},{10,9... | collective-permute-start | bytes 393224 | tf_op jit(solution)/shard_map/ppermute | solution.py:500
  10.5 8.6 %copy-start = (bf16[4,2,256,256]{3,2,1,0:T(8,128)(2,1)S(1)}, bf16[4,2,256,256]{3,2,1,0:T(8,128)(2,1)}, u32[]{:S(2)}) copy-start(bf16[4,2,256,256]{3,2,1,0:T(8,128)(2,1)} %constant.121.clone.mats_ref) | copy-start | bytes 3145732
  11.7 6.0 %collective-permute-start.5 = (f32[1,4,16,512]{3,2,1,0:T(8,128)S(1)}, f32[1,4,16,512]{3,2,1,0:T(8,128)S(1)}, u32[]{:S(2)}, u32[]{:S(2)}) collective-permute-start(f32[1,4,16,512]{3,2,1,0:T(8,128)S(1)} %get-tuple-element.6), channel_id=1, source_target_pairs={{0,7},{1,4},{2,5},{3,6},{4,3},{5,0},{6,1},{7,2},{8,15},{9,12},{10,... | collective-permute-start | bytes 393224 | tf_op jit(solution)/shard_map/ppermute | solution.py:500
  13.9 5.2 %collective-permute-start.6 = (f32[1,4,16,512]{3,2,1,0:T(8,128)S(1)}, f32[1,4,16,512]{3,2,1,0:T(8,128)S(1)}, u32[]{:S(2)}, u32[]{:S(2)}) collective-permute-start(f32[1,4,16,512]{3,2,1,0:T(8,128)S(1)} %get-tuple-element.5), channel_id=1, source_target_pairs={{0,1},{1,2},{2,3},{3,0},{4,5},{5,6},{6,7},{7,4},{8,9},{9,10},{10,1... | collective-permute-start | bytes 393224 | tf_op jit(solution)/shard_map/ppermute | solution.py:500
  17.6 1.5 %copy-start.5 = (f32[2,32,128]{2,1,0:T(8,128)S(1)}, f32[2,32,128]{2,1,0:T(8,128)}, u32[]{:S(2)}) copy-start(f32[2,32,128]{2,1,0:T(8,128)} %constant.122.clone.twist_ref) | copy-start | bytes 98308
  20.4 45.7 %copy-start.2 = (f32[2,128,8,128]{3,2,1,0:T(8,128)S(1)}, f32[2,128,8,128]{3,2,1,0:T(8,128)}, u32[]{:S(2)}) copy-start(f32[2,128,8,128]{3,2,1,0:T(8,128)} %constant.124.clone.ahead_ref) | copy-start | bytes 3145732
  20.4 45.7 %copy-start.3 = (bf16[4,256,256]{2,1,0:T(8,128)(2,1)S(1)}, bf16[4,256,256]{2,1,0:T(8,128)(2,1)}, u32[]{:S(2)}) copy-start(bf16[4,256,256]{2,1,0:T(8,128)(2,1)} %constant.123.clone.mats_ref) | copy-start | bytes 1572868
  20.4 45.7 %copy-start.4 = (f32[2,2,2,64,128]{4,3,2,1,0:T(8,128)S(1)}, f32[2,2,2,64,128]{4,3,2,1,0:T(8,128)}, u32[]{:S(2)}) copy-start(f32[2,2,2,64,128]{4,3,2,1,0:T(8,128)} %constant.125.clone.behind_ref) | copy-start | bytes 786436
  20.4 45.7 %copy-start.6 = (f32[2,64,128]{2,1,0:T(8,128)S(1)}, f32[2,64,128]{2,1,0:T(8,128)}, u32[]{:S(2)}) copy-start(f32[2,64,128]{2,1,0:T(8,128)} %constant.126.clone.spin_ref) | copy-start | bytes 196612
  20.4 45.7 %copy-start.7 = (f32[4]{0:T(128)S(1)}, f32[4]{0:T(128)}, u32[]{:S(2)}) copy-start(f32[4]{0:T(128)} %fresnel_ref.1) | copy-start | bytes 52
  20.4 45.7 %copy-start.8 = (f32[2]{0:T(128)S(1)}, f32[2]{0:T(128)}, u32[]{:S(2)}) copy-start(f32[2]{0:T(128)} %terms_ref.1) | copy-start | bytes 28
  66.1 25.0 %copy-start.1 = (bf16[4,2,256,256]{3,2,1,0:T(8,128)(2,1)S(1)}, bf16[4,2,256,256]{3,2,1,0:T(8,128)(2,1)}, u32[]{:S(2)}) copy-start(bf16[4,2,256,256]{3,2,1,0:T(8,128)(2,1)} %constant.127.clone.mats_ref) | copy-start | bytes 3145732

commit v6 on v5

--- a/solution.py
+++ b/solution.py
@@ -487,9 +487,7 @@
 
 def ring_exchange(field):
     me = lax.axis_index("col")
-    own = lax.dynamic_slice_in_dim(field, me, 1, 1)
     result = jnp.zeros((8, 4, 16, 512), F32)
-    result = lax.dynamic_update_slice_in_dim(result, own.transpose(1, 0, 2, 3), me, 0)
     for step, flip in STEPS:
 
         def there(place, sign):
@@ -499,6 +497,9 @@
         pairs = [(place, there(place, 1)) for place in range(8)]
         chunk = lax.ppermute(chunk.reshape(1, 4, 16, 512), "col", pairs)
         result = lax.dynamic_update_slice_in_dim(result, chunk, there(me, -1), 0)
+        if (step, flip) == STEPS[2]:
+            own = lax.dynamic_slice_in_dim(field, me, 1, 1)
+            result = lax.dynamic_update_slice_in_dim(result, own.transpose(1, 0, 2, 3), me, 0)
     return result
 
 

time: 102 us -> 101 us (level)
  transfers between devices with their start and end apart: 7 -> 7, of which waited for: 3 -> 2; matrix products, arithmetic and copies ran while one was open for 2% -> 1% of each run, Pallas kernels for 0% -> 0%
where the time goes in v6:
time: 101 us
  blocking collectives  75.7 us (75%)
  starting transfers between devices  11.6 us (11%)
  Pallas kernels  5.5 us (5%)
  waiting for transfers between devices  4.71 us (5%)
  local copies, waits for them, and re-layouts  3.25 us (3%)
    all_to_all x2, blocking collectives, exchange_all(): lax.all_to_all(field, ('row', 'col'), split_axis=0, concat_axis=0, tiled=...  66.8 us
    ppermute x7, starting transfers between devices, ring_exchange(): chunk = lax.ppermute(chunk.reshape(1, 4, 16, 512), 'col', pairs)  11.6 us
    all_to_all x1, blocking collectives, exchange(): return lax.all_to_all(field, 'col', split_axis=0, concat_axis=0, tiled=True)  8.95 us
    pallas_call x3, Pallas kernels, call(): pl.pallas_call(kernel, out_shape=jax.ShapeDtypeStruct(out_shape, F32), in...  5.5 us
    ppermute x7, waiting for transfers between devices, ring_exchange(): chunk = lax.ppermute(chunk.reshape(1, 4, 16, 512), 'col', pairs)  4.71 us
  transfers between devices with their start and end apart: 7, of which 2 were waited for; matrix products, arithmetic and copies ran while one was open for 1% of the time, Pallas kernels for 0%

profile of v6, /device:TPU:1, one launch (start us, length us, event | category | flops | bytes accessed | tf_op | source)
XLA Modules:
  0.0 101.0 jit_solution(14198601179915611750)
XLA Ops:
  0.0 1.3 %dynamic-slice_bitcast_fusion = (f32[1,4,16,512]{3,2,1,0:T(8,128)S(1)}, f32[1,4,16,512]{3,2,1,0:T(8,128)S(1)}, f32[1,4,16,512]{3,2,1,0:T(8,128)S(1)}, f32[1,4,16...) fusion(f32[4,8,16,512]{3,2,1,0:T(8,128)} %bitcast.38, ...), kind=kLoop, calls=%fused_computation.1 | loop fusion | bytes 1835036 | tf_op jit(solution)/shard_map/reshape | solution.py:498
  1.3 5.0 %collective-permute-start = (f32[1,4,16,512]{3,2,1,0:T(8,128)S(1)}, f32[1,4,16,512]{3,2,1,0:T(8,128)S(1)}, u32[]{:S(2)}, u32[]{:S(2)}) collective-permute-start(f32[1,4,16,512]{3,2,1,0:T(8,128)S(1)} %get-tuple-element.11), channel_id=1, source_target_pairs={{0,6},{1,7},{2,4},{3,5},{4,2},{5,3},{6,0},{7,1},{8,14},{9,15},{10,... | collective-permute-start | bytes 393224 | tf_op jit(solution)/shard_map/ppermute | solution.py:498
  6.3 0.0 collective-permute-start.1
  6.3 0.4 collective-permute-start.2
  6.7 2.2 %collective-permute-start.3 = (f32[1,4,16,512]{3,2,1,0:T(8,128)S(1)}, f32[1,4,16,512]{3,2,1,0:T(8,128)S(1)}, u32[]{:S(2)}, u32[]{:S(2)}) collective-permute-start(f32[1,4,16,512]{3,2,1,0:T(8,128)S(1)} %get-tuple-element.8), channel_id=1, source_target_pairs={{0,5},{1,6},{2,7},{3,4},{4,1},{5,2},{6,3},{7,0},{8,13},{9,14},{10,... | collective-permute-start | bytes 393224 | tf_op jit(solution)/shard_map/ppermute | solution.py:498
  9.0 1.5 %collective-permute-start.4 = (f32[1,4,16,512]{3,2,1,0:T(8,128)S(1)}, f32[1,4,16,512]{3,2,1,0:T(8,128)S(1)}, u32[]{:S(2)}, u32[]{:S(2)}) collective-permute-start(f32[1,4,16,512]{3,2,1,0:T(8,128)S(1)} %get-tuple-element.7), channel_id=1, source_target_pairs={{0,3},{1,0},{2,1},{3,2},{4,7},{5,4},{6,5},{7,6},{8,11},{9,8},{10,9... | collective-permute-start | bytes 393224 | tf_op jit(solution)/shard_map/ppermute | solution.py:498
  10.4 0.0 collective-permute-done
  10.4 2.4 %collective-permute-start.5 = (f32[1,4,16,512]{3,2,1,0:T(8,128)S(1)}, f32[1,4,16,512]{3,2,1,0:T(8,128)S(1)}, u32[]{:S(2)}, u32[]{:S(2)}) collective-permute-start(f32[1,4,16,512]{3,2,1,0:T(8,128)S(1)} %get-tuple-element.6), channel_id=1, source_target_pairs={{0,7},{1,4},{2,5},{3,6},{4,3},{5,0},{6,1},{7,2},{8,15},{9,12},{10,... | collective-permute-start | bytes 393224 | tf_op jit(solution)/shard_map/ppermute | solution.py:498
  12.8 0.1 broadcast_in_dim.3
  13.0 0.0 copy-start
  13.0 0.0 collective-permute-done.1
  13.0 0.1 collective-permute-start.6
  13.1 4.0 %collective-permute-done.2 = f32[1,4,16,512]{3,2,1,0:T(8,128)S(1)} collective-permute-done((f32[1,4,16,512]{3,2,1,0:T(8,128)S(1)}, f32[1,4,16,512]{3,2,1,0:T(8,128)S(1)}, u32[]{:S(2)}, u32[]{:S(2)}) %collective-permute-start.2) | collective-permute-done | bytes 131104 | tf_op jit(solution)/shard_map/ppermute | solution.py:498
  17.1 0.9 bitcast_dynamic-update-slice_fusion
  18.1 0.0 collective-permute-done.3
  18.1 0.0 collective-permute-done.4
  18.1 0.0 collective-permute-done.5
  18.2 0.0 copy-start.5
  18.2 0.7 collective-permute-done.6
  18.9 0.0 copy-done
  18.9 0.0 copy-done.5
  18.9 1.2 %shard_map.109 = f32[256,8,128]{2,1,0:T(8,128)S(1)} custom-call(f32[8,4,16,512]{3,2,1,0:T(8,128)S(1)} %constant_dynamic-update-slice_fusion.3.field_ref, bf16[4,2,256,256]{3,2,1,0:T(8,128)(2,1)S(1)} %copy-done, f32[2,32,128]{2,1,0:T(8,128)S(1)} %copy-done.5), custom_call_target="tpu_custom_call" | custom-call | tf_op jit(solution)/shard_map/pallas_call | solution.py:456
  20.2 0.0 copy-start.2
  20.2 0.0 copy-start.3
  20.2 0.0 copy-start.4
  20.2 0.0 copy-start.6
  20.2 0.0 copy-start.7
  20.2 0.0 copy-start.8
  20.2 45.5 %all_to_all.15.field_ref = f32[256,8,128]{2,1,0:T(8,128)S(1)} all-to-all(f32[256,8,128]{2,1,0:T(8,128)S(1)} %shard_map.109), channel_id=1, replica_groups={{0,128,1,129,2,130,3,131,4,132,5,133,6,134,7,135,8,136,9,137,10,138,11,..., dimensions={0} | all-to-all | bytes 2097152 | tf_op jit(solution)/shard_map/all_to_all | solution.py:511
  65.7 0.0 copy-done.2
  65.7 0.0 copy-done.3
  65.8 0.0 copy-done.4
  65.8 0.0 copy-done.6
  65.8 0.0 copy-done.7
  65.8 0.0 copy-done.8
  65.8 0.0 copy-start.1
  65.8 3.7 %shard_map.110 = f32[64,8,128]{2,1,0:T(8,128)S(1)} custom-call(f32[4]{0:T(128)S(1)} %copy-done.7, f32[2]{0:T(128)S(1)} %copy-done.8, f32[256,8,128]{2,1,0:T(8,128)S(1)} %all_to_all.15.field_ref, bf16[4,256,256]{2,1,0:T(8,128)(2,1)S(1)} %copy-done.3, f32[2,128,8,128]{3,2,1,0:T(8,128)S(1)} %copy-done.2, f32[2,2,2,64,128]{4,3,2,1,0:T(8,128)S(1)} %copy-done.4, ...), custom_call_target="tpu_custom_call" | custom-call | tf_op jit(solution)/shard_map/pallas_call | solution.py:456
  69.5 21.3 %all_to_all.16 = f32[256,2,128]{2,1,0:T(2,128)S(1)} all-to-all(f32[256,2,128]{2,1,0:T(2,128)S(1)} %bitcast.36), channel_id=1, replica_groups={{0,128,1,129,2,130,3,131,4,132,5,133,6,134,7,135,8,136,9,137,10,138,11,..., dimensions={0} | all-to-all | bytes 524288 | tf_op jit(solution)/shard_map/all_to_all | solution.py:511
  90.7 0.0 copy-done.1
  90.7 0.6 shard_map.111
  91.4 8.9 %all_to_all.17 = f32[8,16,512]{2,1,0:T(8,128)S(1)} all-to-all(f32[8,16,512]{2,1,0:T(8,128)S(1)} %shard_map.111), channel_id=1, replica_groups=mesh['row'=32,'col'=8] {'col'}, dimensions={0} | all-to-all | bytes 524288 | tf_op jit(solution)/shard_map/all_to_all | solution.py:507
  100.3 0.7 copy.37
  (7 shorter events, 0.1 us)
Async XLA Ops:
  1.3 9.1 %collective-permute-start = (f32[1,4,16,512]{3,2,1,0:T(8,128)S(1)}, f32[1,4,16,512]{3,2,1,0:T(8,128)S(1)}, u32[]{:S(2)}, u32[]{:S(2)}) collective-permute-start(f32[1,4,16,512]{3,2,1,0:T(8,128)S(1)} %get-tuple-element.11), channel_id=1, source_target_pairs={{0,6},{1,7},{2,4},{3,5},{4,2},{5,3},{6,0},{7,1},{8,14},{9,15},{10,... | collective-permute-start | bytes 393224 | tf_op jit(solution)/shard_map/ppermute | solution.py:498
  6.3 6.7 %collective-permute-start.1 = (f32[1,4,16,512]{3,2,1,0:T(8,128)S(1)}, f32[1,4,16,512]{3,2,1,0:T(8,128)S(1)}, u32[]{:S(2)}, u32[]{:S(2)}) collective-permute-start(f32[1,4,16,512]{3,2,1,0:T(8,128)S(1)} %get-tuple-element.10), channel_id=1, source_target_pairs={{0,4},{1,5},{2,6},{3,7},{4,0},{5,1},{6,2},{7,3},{8,12},{9,13},{10,... | collective-permute-start | bytes 393224 | tf_op jit(solution)/shard_map/ppermute | solution.py:498
  6.3 10.8 %collective-permute-start.2 = (f32[1,4,16,512]{3,2,1,0:T(8,128)S(1)}, f32[1,4,16,512]{3,2,1,0:T(8,128)S(1)}, u32[]{:S(2)}, u32[]{:S(2)}) collective-permute-start(f32[1,4,16,512]{3,2,1,0:T(8,128)S(1)} %get-tuple-element.9), channel_id=1, source_target_pairs={{0,2},{1,3},{2,0},{3,1},{4,6},{5,7},{6,4},{7,5},{8,10},{9,11},{10,... | collective-permute-start | bytes 393224 | tf_op jit(solution)/shard_map/ppermute | solution.py:498
  6.7 11.4 %collective-permute-start.3 = (f32[1,4,16,512]{3,2,1,0:T(8,128)S(1)}, f32[1,4,16,512]{3,2,1,0:T(8,128)S(1)}, u32[]{:S(2)}, u32[]{:S(2)}) collective-permute-start(f32[1,4,16,512]{3,2,1,0:T(8,128)S(1)} %get-tuple-element.8), channel_id=1, source_target_pairs={{0,5},{1,6},{2,7},{3,4},{4,1},{5,2},{6,3},{7,0},{8,13},{9,14},{10,... | collective-permute-start | bytes 393224 | tf_op jit(solution)/shard_map/ppermute | solution.py:498
  9.0 9.2 %collective-permute-start.4 = (f32[1,4,16,512]{3,2,1,0:T(8,128)S(1)}, f32[1,4,16,512]{3,2,1,0:T(8,128)S(1)}, u32[]{:S(2)}, u32[]{:S(2)}) collective-permute-start(f32[1,4,16,512]{3,2,1,0:T(8,128)S(1)} %get-tuple-element.7), channel_id=1, source_target_pairs={{0,3},{1,0},{2,1},{3,2},{4,7},{5,4},{6,5},{7,6},{8,11},{9,8},{10,9... | collective-permute-start | bytes 393224 | tf_op jit(solution)/shard_map/ppermute | solution.py:498
  10.4 7.7 %collective-permute-start.5 = (f32[1,4,16,512]{3,2,1,0:T(8,128)S(1)}, f32[1,4,16,512]{3,2,1,0:T(8,128)S(1)}, u32[]{:S(2)}, u32[]{:S(2)}) collective-permute-start(f32[1,4,16,512]{3,2,1,0:T(8,128)S(1)} %get-tuple-element.6), channel_id=1, source_target_pairs={{0,7},{1,4},{2,5},{3,6},{4,3},{5,0},{6,1},{7,2},{8,15},{9,12},{10,... | collective-permute-start | bytes 393224 | tf_op jit(solution)/shard_map/ppermute | solution.py:498
  13.0 5.9 %copy-start = (bf16[4,2,256,256]{3,2,1,0:T(8,128)(2,1)S(1)}, bf16[4,2,256,256]{3,2,1,0:T(8,128)(2,1)}, u32[]{:S(2)}) copy-start(bf16[4,2,256,256]{3,2,1,0:T(8,128)(2,1)} %constant.121.clone.mats_ref) | copy-start | bytes 3145732
  13.0 5.9 %collective-permute-start.6 = (f32[1,4,16,512]{3,2,1,0:T(8,128)S(1)}, f32[1,4,16,512]{3,2,1,0:T(8,128)S(1)}, u32[]{:S(2)}, u32[]{:S(2)}) collective-permute-start(f32[1,4,16,512]{3,2,1,0:T(8,128)S(1)} %get-tuple-element.5), channel_id=1, source_target_pairs={{0,1},{1,2},{2,3},{3,0},{4,5},{5,6},{6,7},{7,4},{8,9},{9,10},{10,1... | collective-permute-start | bytes 393224 | tf_op jit(solution)/shard_map/ppermute | solution.py:498
  18.2 0.8 copy-start.5
  20.2 45.6 %copy-start.2 = (f32[2,128,8,128]{3,2,1,0:T(8,128)S(1)}, f32[2,128,8,128]{3,2,1,0:T(8,128)}, u32[]{:S(2)}) copy-start(f32[2,128,8,128]{3,2,1,0:T(8,128)} %constant.124.clone.ahead_ref) | copy-start | bytes 3145732
  20.2 45.6 %copy-start.3 = (bf16[4,256,256]{2,1,0:T(8,128)(2,1)S(1)}, bf16[4,256,256]{2,1,0:T(8,128)(2,1)}, u32[]{:S(2)}) copy-start(bf16[4,256,256]{2,1,0:T(8,128)(2,1)} %constant.123.clone.mats_ref) | copy-start | bytes 1572868
  20.2 45.6 %copy-start.4 = (f32[2,2,2,64,128]{4,3,2,1,0:T(8,128)S(1)}, f32[2,2,2,64,128]{4,3,2,1,0:T(8,128)}, u32[]{:S(2)}) copy-start(f32[2,2,2,64,128]{4,3,2,1,0:T(8,128)} %constant.125.clone.behind_ref) | copy-start | bytes 786436
  20.2 45.6 %copy-start.6 = (f32[2,64,128]{2,1,0:T(8,128)S(1)}, f32[2,64,128]{2,1,0:T(8,128)}, u32[]{:S(2)}) copy-start(f32[2,64,128]{2,1,0:T(8,128)} %constant.126.clone.spin_ref) | copy-start | bytes 196612
  20.2 45.6 %copy-start.7 = (f32[4]{0:T(128)S(1)}, f32[4]{0:T(128)}, u32[]{:S(2)}) copy-start(f32[4]{0:T(128)} %fresnel_ref.1) | copy-start | bytes 52
  20.2 45.6 %copy-start.8 = (f32[2]{0:T(128)S(1)}, f32[2]{0:T(128)}, u32[]{:S(2)}) copy-start(f32[2]{0:T(128)} %terms_ref.1) | copy-start | bytes 28
  65.8 25.0 %copy-start.1 = (bf16[4,2,256,256]{3,2,1,0:T(8,128)(2,1)S(1)}, bf16[4,2,256,256]{3,2,1,0:T(8,128)(2,1)}, u32[]{:S(2)}) copy-start(bf16[4,2,256,256]{3,2,1,0:T(8,128)(2,1)} %constant.127.clone.mats_ref) | copy-start | bytes 3145732

commit v7 on v4

--- a/solution.py
+++ b/solution.py
@@ -173,7 +173,12 @@
     return one(left[0], right[0]) + (one(left[0], right[1]) + one(left[1], right[0]))
 
 
-def rows_kernel(field_ref, mats_ref, twist_ref, out_ref, high_ref, low_ref):
+def rows_kernel(*refs):
+    chunk_refs = refs[:8]
+    mats_ref, twist_ref, out_ref, high_ref, low_ref, field_ref = refs[8:]
+    me = column_number()
+    for (step, flip), chunk_ref in zip(STEPS + [(0, 0)], chunk_refs):
+        field_ref[there(me, -step, flip)] = chunk_ref[...]
     for j in range(2):
         lines = []
         for n1 in range(32):
@@ -229,6 +234,10 @@
 
 
 SINE = sine_fit()
+
+
+def column_number():
+    return lax.axis_index("col")
 
 
 def device_number():
@@ -463,10 +472,11 @@
     )(*arguments)
 
 
-def image_rows(field):
-    arguments = [field] + [jnp.asarray(c) for c in row_constants()]
+def image_rows(chunks):
+    arguments = chunks + [jnp.asarray(c) for c in row_constants()]
     scratch = [pltpu.VMEM((1024, 256), BF16), pltpu.VMEM((1024, 256), BF16)]
-    return call(rows_kernel, (256, 8, 128), scratch, arguments, [pltpu.VMEM] * 3)
+    scratch.append(pltpu.VMEM((8, 4, 16, 512), F32))
+    return call(rows_kernel, (256, 8, 128), scratch, arguments, [pltpu.VMEM] * 10)
 
 
 def filter_columns(field, fresnel, ctf_terms):
@@ -482,6 +492,24 @@
     return call(image_kernel, (8, 16, 512), [], arguments, [pltpu.VMEM] * 3)
 
 
+STEPS = [(2, 1), (0, 1), (2, 0), (1, 1), (3, 0), (3, 1), (1, 0)]
+
+
+def there(place, step, flip):
+    return (place // 4 ^ flip) * 4 + (place + step + 4) % 4
+
+
+def ring_exchange(field):
+    me = lax.axis_index("col")
+    chunks = []
+    for step, flip in STEPS:
+        chunk = lax.dynamic_slice_in_dim(field, there(me, step, flip), 1, 1)
+        pairs = [(place, there(place, step, flip)) for place in range(8)]
+        chunks.append(lax.ppermute(chunk.reshape(4, 16, 512), "col", pairs))
+    own = lax.dynamic_slice_in_dim(field, me, 1, 1)
+    return chunks + [own.reshape(4, 16, 512)]
+
+
 def exchange(field):
     return lax.all_to_all(field, "col", split_axis=0, concat_axis=0, tiled=True)
 
@@ -493,8 +521,7 @@
 
 
 def local(holograms, fresnel, ctf_terms):
-    field = holograms.reshape(4, 8, 16, 512).transpose(1, 0, 2, 3)
-    field = image_rows(exchange(field))
+    field = image_rows(ring_exchange(holograms.reshape(4, 8, 16, 512)))
     field = filter_columns(exchange_all(field), fresnel, ctf_terms)
     field = exchange_all(field.reshape(256, 2, 128))
     image = image_from(field.reshape(512, 128))

time: 103 us -> 101 us (0.981)
  blocking collectives: 95 us -> 76.5 us
  starting transfers between devices: 0 us -> 10.7 us
  waiting for transfers between devices: 0 us -> 5.56 us
    all_to_all x2 -> x1, blocking collectives: 29.4 us -> 8.95 us  [exchange(): return lax.all_to_all(field, 'col', split_axis=0, concat_axis=0, tiled=True)]
    ppermute x0 -> x7, starting transfers between devices: none -> 10.7 us  [ring_exchange(): chunks.append(lax.ppermute(chunk.reshape(4, 16, 512), 'col', pairs))]
    ppermute x0 -> x7, waiting for transfers between devices: none -> 5.56 us  [ring_exchange(): chunks.append(lax.ppermute(chunk.reshape(4, 16, 512), 'col', pairs))]
    all_to_all x2, blocking collectives: 65.6 us -> 67.5 us  [exchange_all(): lax.all_to_all(field, ('row', 'col'), split_axis=0, concat_axis=0, tiled=...]
  transfers between devices with their start and end apart: 0 -> 7, of which waited for: 0 -> 5; matrix products, arithmetic and copies ran while one was open for 0% -> 0% of each run, Pallas kernels for 0% -> 0%
where the time goes in v7:
time: 101 us
  blocking collectives  76.5 us (76%)
  starting transfers between devices  10.7 us (11%)
  Pallas kernels  5.63 us (6%)
  waiting for transfers between devices  5.56 us (6%)
  local copies, waits for them, and re-layouts  2.23 us (2%)
    all_to_all x2, blocking collectives, exchange_all(): lax.all_to_all(field, ('row', 'col'), split_axis=0, concat_axis=0, tiled=...  67.5 us
    ppermute x7, starting transfers between devices, ring_exchange(): chunks.append(lax.ppermute(chunk.reshape(4, 16, 512), 'col', pairs))  10.7 us
    all_to_all x1, blocking collectives, exchange(): return lax.all_to_all(field, 'col', split_axis=0, concat_axis=0, tiled=True)  8.95 us
    pallas_call x3, Pallas kernels, call(): pl.pallas_call(kernel, out_shape=jax.ShapeDtypeStruct(out_shape, F32), in...  5.63 us
    ppermute x7, waiting for transfers between devices, ring_exchange(): chunks.append(lax.ppermute(chunk.reshape(4, 16, 512), 'col', pairs))  5.56 us
  transfers between devices with their start and end apart: 7, of which 5 were waited for; matrix products, arithmetic and copies ran while one was open for 0% of the time, Pallas kernels for 0%

profile of v7, /device:TPU:1, one launch (start us, length us, event | category | flops | bytes accessed | tf_op | source)
XLA Modules:
  0.0 100.7 jit_solution(16802207791549797980)
XLA Ops:
  0.0 0.0 copy-start
  0.0 0.0 copy-start.5
  0.0 1.5 %dynamic-slice_bitcast_fusion = (f32[4,16,512]{2,1,0:T(8,128)S(1)}, f32[4,16,512]{2,1,0:T(8,128)S(1)}, f32[4,16,512]{2,1,0:T(8,128)S(1)}, f32[4,16,512]{2,1,0:T(...) fusion(f32[4,8,16,512]{3,2,1,0:T(8,128)} %bitcast.38, ...), kind=kLoop, calls=%fused_computation | loop fusion | bytes 2097184 | tf_op jit(solution)/shard_map/reshape | solution.py:510
  1.5 2.1 %collective-permute-start.6 = (f32[4,16,512]{2,1,0:T(8,128)S(1)}, f32[4,16,512]{2,1,0:T(8,128)S(1)}, u32[]{:S(2)}, u32[]{:S(2)}) collective-permute-start(f32[4,16,512]{2,1,0:T(8,128)S(1)} %get-tuple-element.6), channel_id=1, source_target_pairs={{0,1},{1,2},{2,3},{3,0},{4,5},{5,6},{6,7},{7,4},{8,9},{9,10},{10,1... | collective-permute-start | bytes 393224 | tf_op jit(solution)/shard_map/ppermute | solution.py:508
  3.6 2.8 %collective-permute-start.5 = (f32[4,16,512]{2,1,0:T(8,128)S(1)}, f32[4,16,512]{2,1,0:T(8,128)S(1)}, u32[]{:S(2)}, u32[]{:S(2)}) collective-permute-start(f32[4,16,512]{2,1,0:T(8,128)S(1)} %get-tuple-element.7), channel_id=1, source_target_pairs={{0,7},{1,4},{2,5},{3,6},{4,3},{5,0},{6,1},{7,2},{8,15},{9,12},{10,... | collective-permute-start | bytes 393224 | tf_op jit(solution)/shard_map/ppermute | solution.py:508
  6.4 1.3 %collective-permute-start.4 = (f32[4,16,512]{2,1,0:T(8,128)S(1)}, f32[4,16,512]{2,1,0:T(8,128)S(1)}, u32[]{:S(2)}, u32[]{:S(2)}) collective-permute-start(f32[4,16,512]{2,1,0:T(8,128)S(1)} %get-tuple-element.8), channel_id=1, source_target_pairs={{0,3},{1,0},{2,1},{3,2},{4,7},{5,4},{6,5},{7,6},{8,11},{9,8},{10,9... | collective-permute-start | bytes 393224 | tf_op jit(solution)/shard_map/ppermute | solution.py:508
  7.7 0.0 collective-permute-start.3
  7.7 1.3 %collective-permute-start.2 = (f32[4,16,512]{2,1,0:T(8,128)S(1)}, f32[4,16,512]{2,1,0:T(8,128)S(1)}, u32[]{:S(2)}, u32[]{:S(2)}) collective-permute-start(f32[4,16,512]{2,1,0:T(8,128)S(1)} %get-tuple-element.10), channel_id=1, source_target_pairs={{0,2},{1,3},{2,0},{3,1},{4,6},{5,7},{6,4},{7,5},{8,10},{9,11},{10,... | collective-permute-start | bytes 393224 | tf_op jit(solution)/shard_map/ppermute | solution.py:508
  9.0 0.0 collective-permute-done.6.refs_6_
  9.0 1.6 %collective-permute-start.1 = (f32[4,16,512]{2,1,0:T(8,128)S(1)}, f32[4,16,512]{2,1,0:T(8,128)S(1)}, u32[]{:S(2)}, u32[]{:S(2)}) collective-permute-start(f32[4,16,512]{2,1,0:T(8,128)S(1)} %get-tuple-element.11), channel_id=1, source_target_pairs={{0,4},{1,5},{2,6},{3,7},{4,0},{5,1},{6,2},{7,3},{8,12},{9,13},{10,... | collective-permute-start | bytes 393224 | tf_op jit(solution)/shard_map/ppermute | solution.py:508
  10.6 0.0 collective-permute-done.5.refs_5_
  10.6 1.6 %collective-permute-start = (f32[4,16,512]{2,1,0:T(8,128)S(1)}, f32[4,16,512]{2,1,0:T(8,128)S(1)}, u32[]{:S(2)}, u32[]{:S(2)}) collective-permute-start(f32[4,16,512]{2,1,0:T(8,128)S(1)} %get-tuple-element.12), channel_id=1, source_target_pairs={{0,6},{1,7},{2,4},{3,5},{4,2},{5,3},{6,0},{7,1},{8,14},{9,15},{10,... | collective-permute-start | bytes 393224 | tf_op jit(solution)/shard_map/ppermute | solution.py:508
  12.2 0.4 collective-permute-done.4.refs_4_
  12.6 1.6 %collective-permute-done.3.refs_3_ = f32[4,16,512]{2,1,0:T(8,128)S(1)} collective-permute-done((f32[4,16,512]{2,1,0:T(8,128)S(1)}, f32[4,16,512]{2,1,0:T(8,128)S(1)}, u32[]{:S(2)}, u32[]{:S(2)}) %collective-permute-start.3) | collective-permute-done | bytes 131104 | tf_op jit(solution)/shard_map/ppermute | solution.py:508
  14.2 1.1 %collective-permute-done.2.refs_2_ = f32[4,16,512]{2,1,0:T(8,128)S(1)} collective-permute-done((f32[4,16,512]{2,1,0:T(8,128)S(1)}, f32[4,16,512]{2,1,0:T(8,128)S(1)}, u32[]{:S(2)}, u32[]{:S(2)}) %collective-permute-start.2) | collective-permute-done | bytes 131104 | tf_op jit(solution)/shard_map/ppermute | solution.py:508
  15.4 0.2 collective-permute-done.1.refs_1_
  15.6 2.2 %collective-permute-done.refs_0_ = f32[4,16,512]{2,1,0:T(8,128)S(1)} collective-permute-done((f32[4,16,512]{2,1,0:T(8,128)S(1)}, f32[4,16,512]{2,1,0:T(8,128)S(1)}, u32[]{:S(2)}, u32[]{:S(2)}) %collective-permute-start) | collective-permute-done | bytes 131104 | tf_op jit(solution)/shard_map/ppermute | solution.py:508
  17.8 0.0 copy-done
  17.8 0.0 copy-done.5
  17.8 1.3 %shard_map.109 = f32[256,8,128]{2,1,0:T(8,128)S(1)} custom-call(f32[4,16,512]{2,1,0:T(8,128)S(1)} %collective-permute-done.refs_0_, f32[4,16,512]{2,1,0:T(8,128)S(1)} %collective-permute-done.1.refs_1_, f32[4,16,512]{2,1,0:T(8,128)S(1)} %collective-permute-done.2.refs_2_, f32[4,16,512]{2,1,0:T(8,128)S(1)} %collective-permute-done.3.refs_3_, ...), custom_call_target="tpu_custom_call" | custom-call | tf_op jit(solution)/shard_map/pallas_call | solution.py:465
  19.1 0.0 copy-start.2
  19.1 0.0 copy-start.3
  19.1 0.0 copy-start.4
  19.1 0.0 copy-start.6
  19.1 0.0 copy-start.7
  19.1 0.0 copy-start.8
  19.2 46.3 %all_to_all.15.field_ref = f32[256,8,128]{2,1,0:T(8,128)S(1)} all-to-all(f32[256,8,128]{2,1,0:T(8,128)S(1)} %shard_map.109), channel_id=1, replica_groups={{0,128,1,129,2,130,3,131,4,132,5,133,6,134,7,135,8,136,9,137,10,138,11,..., dimensions={0} | all-to-all | bytes 2097152 | tf_op jit(solution)/shard_map/all_to_all | solution.py:518
  65.4 0.0 copy-done.2
  65.4 0.0 copy-done.3
  65.4 0.0 copy-done.4
  65.4 0.0 copy-done.6
  65.4 0.0 copy-done.7
  65.4 0.0 copy-done.8
  65.5 0.0 copy-start.1
  65.5 3.7 %shard_map.110 = f32[64,8,128]{2,1,0:T(8,128)S(1)} custom-call(f32[4]{0:T(128)S(1)} %copy-done.7, f32[2]{0:T(128)S(1)} %copy-done.8, f32[256,8,128]{2,1,0:T(8,128)S(1)} %all_to_all.15.field_ref, bf16[4,256,256]{2,1,0:T(8,128)(2,1)S(1)} %copy-done.3, f32[2,128,8,128]{3,2,1,0:T(8,128)S(1)} %copy-done.2, f32[2,2,2,64,128]{4,3,2,1,0:T(8,128)S(1)} %copy-done.4, ...), custom_call_target="tpu_custom_call" | custom-call | tf_op jit(solution)/shard_map/pallas_call | solution.py:465
  69.2 21.3 %all_to_all.16 = f32[256,2,128]{2,1,0:T(2,128)S(1)} all-to-all(f32[256,2,128]{2,1,0:T(2,128)S(1)} %bitcast.36), channel_id=1, replica_groups={{0,128,1,129,2,130,3,131,4,132,5,133,6,134,7,135,8,136,9,137,10,138,11,..., dimensions={0} | all-to-all | bytes 524288 | tf_op jit(solution)/shard_map/all_to_all | solution.py:518
  90.5 0.0 copy-done.1
  90.5 0.6 shard_map.111
  91.1 9.0 %all_to_all.17 = f32[8,16,512]{2,1,0:T(8,128)S(1)} all-to-all(f32[8,16,512]{2,1,0:T(8,128)S(1)} %shard_map.111), channel_id=1, replica_groups=mesh['row'=32,'col'=8] {'col'}, dimensions={0} | all-to-all | bytes 524288 | tf_op jit(solution)/shard_map/all_to_all | solution.py:514
  100.0 0.7 copy.29
Async XLA Ops:
  0.0 17.8 %copy-start = (bf16[4,2,256,256]{3,2,1,0:T(8,128)(2,1)S(1)}, bf16[4,2,256,256]{3,2,1,0:T(8,128)(2,1)}, u32[]{:S(2)}) copy-start(bf16[4,2,256,256]{3,2,1,0:T(8,128)(2,1)} %constant.86.clone.refs_8_) | copy-start | bytes 3145732
  0.0 17.8 %copy-start.5 = (f32[2,32,128]{2,1,0:T(8,128)S(1)}, f32[2,32,128]{2,1,0:T(8,128)}, u32[]{:S(2)}) copy-start(f32[2,32,128]{2,1,0:T(8,128)} %constant.87.clone.refs_9_.twist_ref) | copy-start | bytes 98308
  1.5 7.5 %collective-permute-start.6 = (f32[4,16,512]{2,1,0:T(8,128)S(1)}, f32[4,16,512]{2,1,0:T(8,128)S(1)}, u32[]{:S(2)}, u32[]{:S(2)}) collective-permute-start(f32[4,16,512]{2,1,0:T(8,128)S(1)} %get-tuple-element.6), channel_id=1, source_target_pairs={{0,1},{1,2},{2,3},{3,0},{4,5},{5,6},{6,7},{7,4},{8,9},{9,10},{10,1... | collective-permute-start | bytes 393224 | tf_op jit(solution)/shard_map/ppermute | solution.py:508
  3.6 7.0 %collective-permute-start.5 = (f32[4,16,512]{2,1,0:T(8,128)S(1)}, f32[4,16,512]{2,1,0:T(8,128)S(1)}, u32[]{:S(2)}, u32[]{:S(2)}) collective-permute-start(f32[4,16,512]{2,1,0:T(8,128)S(1)} %get-tuple-element.7), channel_id=1, source_target_pairs={{0,7},{1,4},{2,5},{3,6},{4,3},{5,0},{6,1},{7,2},{8,15},{9,12},{10,... | collective-permute-start | bytes 393224 | tf_op jit(solution)/shard_map/ppermute | solution.py:508
  6.4 6.2 %collective-permute-start.4 = (f32[4,16,512]{2,1,0:T(8,128)S(1)}, f32[4,16,512]{2,1,0:T(8,128)S(1)}, u32[]{:S(2)}, u32[]{:S(2)}) collective-permute-start(f32[4,16,512]{2,1,0:T(8,128)S(1)} %get-tuple-element.8), channel_id=1, source_target_pairs={{0,3},{1,0},{2,1},{3,2},{4,7},{5,4},{6,5},{7,6},{8,11},{9,8},{10,9... | collective-permute-start | bytes 393224 | tf_op jit(solution)/shard_map/ppermute | solution.py:508
  7.7 6.6 %collective-permute-start.3 = (f32[4,16,512]{2,1,0:T(8,128)S(1)}, f32[4,16,512]{2,1,0:T(8,128)S(1)}, u32[]{:S(2)}, u32[]{:S(2)}) collective-permute-start(f32[4,16,512]{2,1,0:T(8,128)S(1)} %get-tuple-element.9), channel_id=1, source_target_pairs={{0,5},{1,6},{2,7},{3,4},{4,1},{5,2},{6,3},{7,0},{8,13},{9,14},{10,... | collective-permute-start | bytes 393224 | tf_op jit(solution)/shard_map/ppermute | solution.py:508
  7.7 7.7 %collective-permute-start.2 = (f32[4,16,512]{2,1,0:T(8,128)S(1)}, f32[4,16,512]{2,1,0:T(8,128)S(1)}, u32[]{:S(2)}, u32[]{:S(2)}) collective-permute-start(f32[4,16,512]{2,1,0:T(8,128)S(1)} %get-tuple-element.10), channel_id=1, source_target_pairs={{0,2},{1,3},{2,0},{3,1},{4,6},{5,7},{6,4},{7,5},{8,10},{9,11},{10,... | collective-permute-start | bytes 393224 | tf_op jit(solution)/shard_map/ppermute | solution.py:508
  9.0 6.6 %collective-permute-start.1 = (f32[4,16,512]{2,1,0:T(8,128)S(1)}, f32[4,16,512]{2,1,0:T(8,128)S(1)}, u32[]{:S(2)}, u32[]{:S(2)}) collective-permute-start(f32[4,16,512]{2,1,0:T(8,128)S(1)} %get-tuple-element.11), channel_id=1, source_target_pairs={{0,4},{1,5},{2,6},{3,7},{4,0},{5,1},{6,2},{7,3},{8,12},{9,13},{10,... | collective-permute-start | bytes 393224 | tf_op jit(solution)/shard_map/ppermute | solution.py:508
  10.6 7.2 %collective-permute-start = (f32[4,16,512]{2,1,0:T(8,128)S(1)}, f32[4,16,512]{2,1,0:T(8,128)S(1)}, u32[]{:S(2)}, u32[]{:S(2)}) collective-permute-start(f32[4,16,512]{2,1,0:T(8,128)S(1)} %get-tuple-element.12), channel_id=1, source_target_pairs={{0,6},{1,7},{2,4},{3,5},{4,2},{5,3},{6,0},{7,1},{8,14},{9,15},{10,... | collective-permute-start | bytes 393224 | tf_op jit(solution)/shard_map/ppermute | solution.py:508
  19.1 46.3 %copy-start.2 = (f32[2,128,8,128]{3,2,1,0:T(8,128)S(1)}, f32[2,128,8,128]{3,2,1,0:T(8,128)}, u32[]{:S(2)}) copy-start(f32[2,128,8,128]{3,2,1,0:T(8,128)} %constant.89.clone.ahead_ref) | copy-start | bytes 3145732
  19.1 46.3 %copy-start.3 = (bf16[4,256,256]{2,1,0:T(8,128)(2,1)S(1)}, bf16[4,256,256]{2,1,0:T(8,128)(2,1)}, u32[]{:S(2)}) copy-start(bf16[4,256,256]{2,1,0:T(8,128)(2,1)} %constant.88.clone.mats_ref) | copy-start | bytes 1572868
  19.1 46.3 %copy-start.4 = (f32[2,2,2,64,128]{4,3,2,1,0:T(8,128)S(1)}, f32[2,2,2,64,128]{4,3,2,1,0:T(8,128)}, u32[]{:S(2)}) copy-start(f32[2,2,2,64,128]{4,3,2,1,0:T(8,128)} %constant.90.clone.behind_ref) | copy-start | bytes 786436
  19.1 46.3 %copy-start.6 = (f32[2,64,128]{2,1,0:T(8,128)S(1)}, f32[2,64,128]{2,1,0:T(8,128)}, u32[]{:S(2)}) copy-start(f32[2,64,128]{2,1,0:T(8,128)} %constant.91.clone.spin_ref) | copy-start | bytes 196612
  19.1 46.3 %copy-start.7 = (f32[4]{0:T(128)S(1)}, f32[4]{0:T(128)}, u32[]{:S(2)}) copy-start(f32[4]{0:T(128)} %fresnel_ref.1) | copy-start | bytes 52
  19.1 46.3 %copy-start.8 = (f32[2]{0:T(128)S(1)}, f32[2]{0:T(128)}, u32[]{:S(2)}) copy-start(f32[2]{0:T(128)} %terms_ref.1) | copy-start | bytes 28
  65.5 25.0 %copy-start.1 = (bf16[4,2,256,256]{3,2,1,0:T(8,128)(2,1)S(1)}, bf16[4,2,256,256]{3,2,1,0:T(8,128)(2,1)}, u32[]{:S(2)}) copy-start(bf16[4,2,256,256]{3,2,1,0:T(8,128)(2,1)} %constant.92.clone.mats_ref) | copy-start | bytes 3145732

commit v8 on v7

--- a/solution.py
+++ b/solution.py
@@ -492,7 +492,7 @@
     return call(image_kernel, (8, 16, 512), [], arguments, [pltpu.VMEM] * 3)
 
 
-STEPS = [(2, 1), (0, 1), (2, 0), (1, 1), (3, 0), (3, 1), (1, 0)]
+STEPS = [(1, 0), (3, 1), (3, 0), (1, 1), (2, 0), (0, 1), (2, 1)]
 
 
 def there(place, step, flip):

time: 101 us -> 101 us (level)
  blocking collectives: 76.5 us -> 75.3 us
    all_to_all x2, blocking collectives: 67.5 us -> 66.3 us  [exchange_all(): lax.all_to_all(field, ('row', 'col'), split_axis=0, concat_axis=0, tiled=...]
  transfers between devices with their start and end apart: 7 -> 7, of which waited for: 5 -> 3; matrix products, arithmetic and copies ran while one was open for 0% -> 0% of each run, Pallas kernels for 0% -> 0%
where the time goes in v8:
time: 101 us
  blocking collectives  75.3 us (75%)
  starting transfers between devices  11.5 us (11%)
  waiting for transfers between devices  6.04 us (6%)
  Pallas kernels  5.64 us (6%)
  local copies, waits for them, and re-layouts  2.23 us (2%)
    all_to_all x2, blocking collectives, exchange_all(): lax.all_to_all(field, ('row', 'col'), split_axis=0, concat_axis=0, tiled=...  66.3 us
    ppermute x7, starting transfers between devices, ring_exchange(): chunks.append(lax.ppermute(chunk.reshape(4, 16, 512), 'col', pairs))  11.5 us
    all_to_all x1, blocking collectives, exchange(): return lax.all_to_all(field, 'col', split_axis=0, concat_axis=0, tiled=True)  8.95 us
    ppermute x7, waiting for transfers between devices, ring_exchange(): chunks.append(lax.ppermute(chunk.reshape(4, 16, 512), 'col', pairs))  6.04 us
    pallas_call x3, Pallas kernels, call(): pl.pallas_call(kernel, out_shape=jax.ShapeDtypeStruct(out_shape, F32), in...  5.64 us
  transfers between devices with their start and end apart: 7, of which 3 were waited for; matrix products, arithmetic and copies ran while one was open for 0% of the time, Pallas kernels for 0%

profile of v8, /device:TPU:1, one launch (start us, length us, event | category | flops | bytes accessed | tf_op | source)
XLA Modules:
  0.0 100.8 jit_solution(7858490024213717547)
XLA Ops:
  0.0 0.0 copy-start
  0.0 0.0 copy-start.5
  0.0 1.5 %dynamic-slice_bitcast_fusion = (f32[4,16,512]{2,1,0:T(8,128)S(1)}, f32[4,16,512]{2,1,0:T(8,128)S(1)}, f32[4,16,512]{2,1,0:T(8,128)S(1)}, f32[4,16,512]{2,1,0:T(...) fusion(f32[4,8,16,512]{3,2,1,0:T(8,128)} %bitcast.38, ...), kind=kLoop, calls=%fused_computation | loop fusion | bytes 2097184 | tf_op jit(solution)/shard_map/reshape | solution.py:510
  1.5 5.0 %collective-permute-start.6 = (f32[4,16,512]{2,1,0:T(8,128)S(1)}, f32[4,16,512]{2,1,0:T(8,128)S(1)}, u32[]{:S(2)}, u32[]{:S(2)}) collective-permute-start(f32[4,16,512]{2,1,0:T(8,128)S(1)} %get-tuple-element.6), channel_id=1, source_target_pairs={{0,6},{1,7},{2,4},{3,5},{4,2},{5,3},{6,0},{7,1},{8,14},{9,15},{10,... | collective-permute-start | bytes 393224 | tf_op jit(solution)/shard_map/ppermute | solution.py:508
  6.5 0.0 collective-permute-start.5
  6.5 0.4 collective-permute-start.4
  6.9 2.2 %collective-permute-start.3 = (f32[4,16,512]{2,1,0:T(8,128)S(1)}, f32[4,16,512]{2,1,0:T(8,128)S(1)}, u32[]{:S(2)}, u32[]{:S(2)}) collective-permute-start(f32[4,16,512]{2,1,0:T(8,128)S(1)} %get-tuple-element.9), channel_id=1, source_target_pairs={{0,5},{1,6},{2,7},{3,4},{4,1},{5,2},{6,3},{7,0},{8,13},{9,14},{10,... | collective-permute-start | bytes 393224 | tf_op jit(solution)/shard_map/ppermute | solution.py:508
  9.1 1.5 %collective-permute-start.2 = (f32[4,16,512]{2,1,0:T(8,128)S(1)}, f32[4,16,512]{2,1,0:T(8,128)S(1)}, u32[]{:S(2)}, u32[]{:S(2)}) collective-permute-start(f32[4,16,512]{2,1,0:T(8,128)S(1)} %get-tuple-element.10), channel_id=1, source_target_pairs={{0,3},{1,0},{2,1},{3,2},{4,7},{5,4},{6,5},{7,6},{8,11},{9,8},{10,9... | collective-permute-start | bytes 393224 | tf_op jit(solution)/shard_map/ppermute | solution.py:508
  10.6 0.0 collective-permute-done.6.refs_6_
  10.6 2.4 %collective-permute-start.1 = (f32[4,16,512]{2,1,0:T(8,128)S(1)}, f32[4,16,512]{2,1,0:T(8,128)S(1)}, u32[]{:S(2)}, u32[]{:S(2)}) collective-permute-start(f32[4,16,512]{2,1,0:T(8,128)S(1)} %get-tuple-element.11), channel_id=1, source_target_pairs={{0,7},{1,4},{2,5},{3,6},{4,3},{5,0},{6,1},{7,2},{8,15},{9,12},{10,... | collective-permute-start | bytes 393224 | tf_op jit(solution)/shard_map/ppermute | solution.py:508
  13.0 0.0 collective-permute-done.5.refs_5_
  13.0 0.0 collective-permute-start
  13.0 4.3 %collective-permute-done.4.refs_4_ = f32[4,16,512]{2,1,0:T(8,128)S(1)} collective-permute-done((f32[4,16,512]{2,1,0:T(8,128)S(1)}, f32[4,16,512]{2,1,0:T(8,128)S(1)}, u32[]{:S(2)}, u32[]{:S(2)}) %collective-permute-start.4) | collective-permute-done | bytes 131104 | tf_op jit(solution)/shard_map/ppermute | solution.py:508
  17.3 0.0 collective-permute-done.3.refs_3_
  17.3 0.0 collective-permute-done.2.refs_2_
  17.3 0.4 collective-permute-done.1.refs_1_
  17.7 1.4 %collective-permute-done.refs_0_ = f32[4,16,512]{2,1,0:T(8,128)S(1)} collective-permute-done((f32[4,16,512]{2,1,0:T(8,128)S(1)}, f32[4,16,512]{2,1,0:T(8,128)S(1)}, u32[]{:S(2)}, u32[]{:S(2)}) %collective-permute-start) | collective-permute-done | bytes 131104 | tf_op jit(solution)/shard_map/ppermute | solution.py:508
  19.0 0.0 copy-done
  19.0 0.0 copy-done.5
  19.0 1.3 %shard_map.109 = f32[256,8,128]{2,1,0:T(8,128)S(1)} custom-call(f32[4,16,512]{2,1,0:T(8,128)S(1)} %collective-permute-done.refs_0_, f32[4,16,512]{2,1,0:T(8,128)S(1)} %collective-permute-done.1.refs_1_, f32[4,16,512]{2,1,0:T(8,128)S(1)} %collective-permute-done.2.refs_2_, f32[4,16,512]{2,1,0:T(8,128)S(1)} %collective-permute-done.3.refs_3_, ...), custom_call_target="tpu_custom_call" | custom-call | tf_op jit(solution)/shard_map/pallas_call | solution.py:465
  20.4 0.0 copy-start.2
  20.4 0.0 copy-start.3
  20.4 0.0 copy-start.4
  20.4 0.0 copy-start.6
  20.4 0.0 copy-start.7
  20.4 0.0 copy-start.8
  20.4 45.1 %all_to_all.15.field_ref = f32[256,8,128]{2,1,0:T(8,128)S(1)} all-to-all(f32[256,8,128]{2,1,0:T(8,128)S(1)} %shard_map.109), channel_id=1, replica_groups={{0,128,1,129,2,130,3,131,4,132,5,133,6,134,7,135,8,136,9,137,10,138,11,..., dimensions={0} | all-to-all | bytes 2097152 | tf_op jit(solution)/shard_map/all_to_all | solution.py:518
  65.5 0.0 copy-done.2
  65.5 0.0 copy-done.3
  65.5 0.0 copy-done.4
  65.5 0.0 copy-done.6
  65.5 0.0 copy-done.7
  65.5 0.0 copy-done.8
  65.5 0.0 copy-start.1
  65.5 3.7 %shard_map.110 = f32[64,8,128]{2,1,0:T(8,128)S(1)} custom-call(f32[4]{0:T(128)S(1)} %copy-done.7, f32[2]{0:T(128)S(1)} %copy-done.8, f32[256,8,128]{2,1,0:T(8,128)S(1)} %all_to_all.15.field_ref, bf16[4,256,256]{2,1,0:T(8,128)(2,1)S(1)} %copy-done.3, f32[2,128,8,128]{3,2,1,0:T(8,128)S(1)} %copy-done.2, f32[2,2,2,64,128]{4,3,2,1,0:T(8,128)S(1)} %copy-done.4, ...), custom_call_target="tpu_custom_call" | custom-call | tf_op jit(solution)/shard_map/pallas_call | solution.py:465
  69.3 21.3 %all_to_all.16 = f32[256,2,128]{2,1,0:T(2,128)S(1)} all-to-all(f32[256,2,128]{2,1,0:T(2,128)S(1)} %bitcast.36), channel_id=1, replica_groups={{0,128,1,129,2,130,3,131,4,132,5,133,6,134,7,135,8,136,9,137,10,138,11,..., dimensions={0} | all-to-all | bytes 524288 | tf_op jit(solution)/shard_map/all_to_all | solution.py:518
  90.5 0.0 copy-done.1
  90.5 0.6 shard_map.111
  91.2 8.9 %all_to_all.17 = f32[8,16,512]{2,1,0:T(8,128)S(1)} all-to-all(f32[8,16,512]{2,1,0:T(8,128)S(1)} %shard_map.111), channel_id=1, replica_groups=mesh['row'=32,'col'=8] {'col'}, dimensions={0} | all-to-all | bytes 524288 | tf_op jit(solution)/shard_map/all_to_all | solution.py:514
  100.1 0.7 copy.29
Async XLA Ops:
  0.0 19.0 %copy-start = (bf16[4,2,256,256]{3,2,1,0:T(8,128)(2,1)S(1)}, bf16[4,2,256,256]{3,2,1,0:T(8,128)(2,1)}, u32[]{:S(2)}) copy-start(bf16[4,2,256,256]{3,2,1,0:T(8,128)(2,1)} %constant.86.clone.refs_8_) | copy-start | bytes 3145732
  0.0 19.0 %copy-start.5 = (f32[2,32,128]{2,1,0:T(8,128)S(1)}, f32[2,32,128]{2,1,0:T(8,128)}, u32[]{:S(2)}) copy-start(f32[2,32,128]{2,1,0:T(8,128)} %constant.87.clone.refs_9_.twist_ref) | copy-start | bytes 98308
  1.5 9.1 %collective-permute-start.6 = (f32[4,16,512]{2,1,0:T(8,128)S(1)}, f32[4,16,512]{2,1,0:T(8,128)S(1)}, u32[]{:S(2)}, u32[]{:S(2)}) collective-permute-start(f32[4,16,512]{2,1,0:T(8,128)S(1)} %get-tuple-element.6), channel_id=1, source_target_pairs={{0,6},{1,7},{2,4},{3,5},{4,2},{5,3},{6,0},{7,1},{8,14},{9,15},{10,... | collective-permute-start | bytes 393224 | tf_op jit(solution)/shard_map/ppermute | solution.py:508
  6.5 6.5 %collective-permute-start.5 = (f32[4,16,512]{2,1,0:T(8,128)S(1)}, f32[4,16,512]{2,1,0:T(8,128)S(1)}, u32[]{:S(2)}, u32[]{:S(2)}) collective-permute-start(f32[4,16,512]{2,1,0:T(8,128)S(1)} %get-tuple-element.7), channel_id=1, source_target_pairs={{0,4},{1,5},{2,6},{3,7},{4,0},{5,1},{6,2},{7,3},{8,12},{9,13},{10,... | collective-permute-start | bytes 393224 | tf_op jit(solution)/shard_map/ppermute | solution.py:508
  6.5 10.8 %collective-permute-start.4 = (f32[4,16,512]{2,1,0:T(8,128)S(1)}, f32[4,16,512]{2,1,0:T(8,128)S(1)}, u32[]{:S(2)}, u32[]{:S(2)}) collective-permute-start(f32[4,16,512]{2,1,0:T(8,128)S(1)} %get-tuple-element.8), channel_id=1, source_target_pairs={{0,2},{1,3},{2,0},{3,1},{4,6},{5,7},{6,4},{7,5},{8,10},{9,11},{10,... | collective-permute-start | bytes 393224 | tf_op jit(solution)/shard_map/ppermute | solution.py:508
  6.9 10.4 %collective-permute-start.3 = (f32[4,16,512]{2,1,0:T(8,128)S(1)}, f32[4,16,512]{2,1,0:T(8,128)S(1)}, u32[]{:S(2)}, u32[]{:S(2)}) collective-permute-start(f32[4,16,512]{2,1,0:T(8,128)S(1)} %get-tuple-element.9), channel_id=1, source_target_pairs={{0,5},{1,6},{2,7},{3,4},{4,1},{5,2},{6,3},{7,0},{8,13},{9,14},{10,... | collective-permute-start | bytes 393224 | tf_op jit(solution)/shard_map/ppermute | solution.py:508
  9.1 8.2 %collective-permute-start.2 = (f32[4,16,512]{2,1,0:T(8,128)S(1)}, f32[4,16,512]{2,1,0:T(8,128)S(1)}, u32[]{:S(2)}, u32[]{:S(2)}) collective-permute-start(f32[4,16,512]{2,1,0:T(8,128)S(1)} %get-tuple-element.10), channel_id=1, source_target_pairs={{0,3},{1,0},{2,1},{3,2},{4,7},{5,4},{6,5},{7,6},{8,11},{9,8},{10,9... | collective-permute-start | bytes 393224 | tf_op jit(solution)/shard_map/ppermute | solution.py:508
  10.6 7.1 %collective-permute-start.1 = (f32[4,16,512]{2,1,0:T(8,128)S(1)}, f32[4,16,512]{2,1,0:T(8,128)S(1)}, u32[]{:S(2)}, u32[]{:S(2)}) collective-permute-start(f32[4,16,512]{2,1,0:T(8,128)S(1)} %get-tuple-element.11), channel_id=1, source_target_pairs={{0,7},{1,4},{2,5},{3,6},{4,3},{5,0},{6,1},{7,2},{8,15},{9,12},{10,... | collective-permute-start | bytes 393224 | tf_op jit(solution)/shard_map/ppermute | solution.py:508
  13.0 6.0 %collective-permute-start = (f32[4,16,512]{2,1,0:T(8,128)S(1)}, f32[4,16,512]{2,1,0:T(8,128)S(1)}, u32[]{:S(2)}, u32[]{:S(2)}) collective-permute-start(f32[4,16,512]{2,1,0:T(8,128)S(1)} %get-tuple-element.12), channel_id=1, source_target_pairs={{0,1},{1,2},{2,3},{3,0},{4,5},{5,6},{6,7},{7,4},{8,9},{9,10},{10,1... | collective-permute-start | bytes 393224 | tf_op jit(solution)/shard_map/ppermute | solution.py:508
  20.4 45.1 %copy-start.2 = (f32[2,128,8,128]{3,2,1,0:T(8,128)S(1)}, f32[2,128,8,128]{3,2,1,0:T(8,128)}, u32[]{:S(2)}) copy-start(f32[2,128,8,128]{3,2,1,0:T(8,128)} %constant.89.clone.ahead_ref) | copy-start | bytes 3145732
  20.4 45.1 %copy-start.3 = (bf16[4,256,256]{2,1,0:T(8,128)(2,1)S(1)}, bf16[4,256,256]{2,1,0:T(8,128)(2,1)}, u32[]{:S(2)}) copy-start(bf16[4,256,256]{2,1,0:T(8,128)(2,1)} %constant.88.clone.mats_ref) | copy-start | bytes 1572868
  20.4 45.1 %copy-start.4 = (f32[2,2,2,64,128]{4,3,2,1,0:T(8,128)S(1)}, f32[2,2,2,64,128]{4,3,2,1,0:T(8,128)}, u32[]{:S(2)}) copy-start(f32[2,2,2,64,128]{4,3,2,1,0:T(8,128)} %constant.90.clone.behind_ref) | copy-start | bytes 786436
  20.4 45.1 %copy-start.6 = (f32[2,64,128]{2,1,0:T(8,128)S(1)}, f32[2,64,128]{2,1,0:T(8,128)}, u32[]{:S(2)}) copy-start(f32[2,64,128]{2,1,0:T(8,128)} %constant.91.clone.spin_ref) | copy-start | bytes 196612
  20.4 45.1 %copy-start.7 = (f32[4]{0:T(128)S(1)}, f32[4]{0:T(128)}, u32[]{:S(2)}) copy-start(f32[4]{0:T(128)} %fresnel_ref.1) | copy-start | bytes 52
  20.4 45.1 %copy-start.8 = (f32[2]{0:T(128)S(1)}, f32[2]{0:T(128)}, u32[]{:S(2)}) copy-start(f32[2]{0:T(128)} %terms_ref.1) | copy-start | bytes 28
  65.5 25.0 %copy-start.1 = (bf16[4,2,256,256]{3,2,1,0:T(8,128)(2,1)S(1)}, bf16[4,2,256,256]{3,2,1,0:T(8,128)(2,1)}, u32[]{:S(2)}) copy-start(bf16[4,2,256,256]{3,2,1,0:T(8,128)(2,1)} %constant.92.clone.mats_ref) | copy-start | bytes 3145732
